TPU v7x, 512 devices: a whole 4x8x8 slice. The times are simulated.
512 devices in a mesh: gx: 8 (over x, core), gy: 8 (over y), gz: 8 (over z).
Axes of the slice: x: 4, y: 8, z: 8, core: 2. Of those that a mesh axis runs over, the one named last changes fastest.
Arguments:
- right_side: float32 [96, 96, 4096], P('gx', 'gy', 'gz'), may hold values from -8 to 8
- phase: int32 [96, 96, 4096], P('gx', 'gy', 'gz'), may hold values 0 or 1
Outputs:
- correction: float32 [96, 96, 4096], P('gx', 'gy', 'gz')
- remainder: float32 [96, 96, 4096], P('gx', 'gy', 'gz')
All inputs are finite; a program needn't handle non-finite values. No bound on the sum of `phase` on one device may be relied on, other than what follows from the above.
Results may differ from a plain program's by a relative error of at most 0.000067.
Values sent between devices are 32-bit elements; how exact they have to be, the bound alone decides.
A program may use at most 128 MiB of HBM per device.

v0:
```python
import jax
import jax.numpy as jnp
from jax import lax
from jax.sharding import PartitionSpec as P

DEGREE = 4
COARSE_ITERS = 8


heavy_density = 20.0
smooth_lowest = 0.3
coarse_lowest = 0.02
upper_bound = 2.0


def with_halo(value, sides, width):
    for axis, dim in sides:
        devices, length = (lax.axis_size(axis), value.shape[dim])
        up = [(i, (i + 1) % devices) for i in range(devices - 1)]
        down = [(j, i) for i, j in up]
        last = lax.slice_in_dim(value, length - width, length, axis=dim)
        leading = lax.slice_in_dim(value, 0, width, axis=dim)
        before = lax.ppermute(last, axis, up)
        after = lax.ppermute(leading, axis, down)
        value = jnp.concatenate([before, value, after], axis=dim)
    return value


def nearby(padded):
    return [
        padded[2:, 1:-1, 1:-1],
        padded[:-2, 1:-1, 1:-1],
        padded[1:-1, 2:, 1:-1],
        padded[1:-1, :-2, 1:-1],
        padded[1:-1, 1:-1, 2:],
        padded[1:-1, 1:-1, :-2],
    ]


def pad_fine(values):
    return with_halo(values, (("gx", 0), ("gy", 1), ("gz", 2)), 1)


def pad_coarse(values):
    return with_halo(values, (("gx", 0), ("gy", 1), ("gz", 2)), 1)


def pad_density(values):
    return with_halo(values, (("gx", 0), ("gy", 1), ("gz", 2)), 1)


def coefficients(density, padded_density, factor):
    facing = [2.0 / (density + other) for other in nearby(padded_density)]
    total = facing[0] + facing[1] + facing[2] + facing[3] + facing[4] + facing[5]
    return (facing, factor * total)


def operate(values, padder, facing, diagonal, factor):
    others = nearby(padder(values))
    summed = facing[0] * others[0]
    for index in range(1, 6):
        summed = summed + facing[index] * others[index]
    return diagonal * values - factor * summed


def chebyshev(initial, residual, facing, diagonal, factor, padder, degree, lowest, finish):
    middle = (upper_bound + lowest) / 2.0
    radius = (upper_bound - lowest) / 2.0
    sharpness = middle / radius
    weight_old = 1.0 / sharpness
    inverse = 1.0 / diagonal
    direction = inverse * residual * (1.0 / middle)
    solution = initial + direction
    residual = residual - operate(direction, padder, facing, diagonal, factor)
    for sweep_index in range(1, degree):
        weight_new = 1.0 / (2.0 * sharpness - weight_old)
        direction = weight_new * weight_old * direction + 2.0 * weight_new / radius * (
            inverse * residual
        )
        solution = solution + direction
        if finish or sweep_index < degree - 1:
            residual = residual - operate(direction, padder, facing, diagonal, factor)
        weight_old = weight_new
    return (solution, residual)


def restrict(values):
    sizes = values.shape
    grouped = values.reshape(sizes[0] // 2, 2, sizes[1] // 2, 2, sizes[2] // 2, 2)
    return jnp.mean(grouped, axis=(1, 3, 5))


def prolong(values):
    return jnp.repeat(jnp.repeat(jnp.repeat(values, 2, 0), 2, 1), 2, 2)


def per_device(right_side, phase):
    density0 = jnp.where(phase == 1, heavy_density, 1.0).astype(jnp.float32)
    facing0, diagonal0 = coefficients(density0, pad_density(density0), 1.0)
    x_first, r_first = chebyshev(
        jnp.zeros_like(right_side),
        right_side,
        facing0,
        diagonal0,
        1.0,
        pad_fine,
        DEGREE,
        smooth_lowest,
        True,
    )
    density1 = restrict(density0)
    facing1, diagonal1 = coefficients(density1, pad_density(density1), 0.25)
    rhs_second = restrict(r_first)
    x_second, r_second = chebyshev(
        jnp.zeros_like(rhs_second),
        rhs_second,
        facing1,
        diagonal1,
        0.25,
        pad_fine,
        DEGREE,
        smooth_lowest,
        True,
    )
    density2 = restrict(density1)
    rhs_third = restrict(r_second)
    padded_coarse = with_halo(density2, (("gx", 0), ("gy", 1), ("gz", 2)), 1)
    facing2, diagonal2 = coefficients(density2, padded_coarse, 0.0625)
    coarse_error, unused = chebyshev(
        jnp.zeros_like(rhs_third),
        rhs_third,
        facing2,
        diagonal2,
        0.0625,
        pad_coarse,
        COARSE_ITERS,
        coarse_lowest,
        False,
    )
    lifted = prolong(coarse_error)
    x_second = x_second + lifted
    r_second = r_second - operate(lifted, pad_fine, facing1, diagonal1, 0.25)
    x_second, r_second = chebyshev(
        x_second, r_second, facing1, diagonal1, 0.25, pad_fine, DEGREE, smooth_lowest, True
    )
    lifted = prolong(x_second)
    x_first = x_first + lifted
    r_first = r_first - operate(lifted, pad_fine, facing0, diagonal0, 1.0)
    x_first, r_first = chebyshev(
        x_first, r_first, facing0, diagonal0, 1.0, pad_fine, DEGREE, smooth_lowest, True
    )
    return (x_first, r_first)


def solution(mesh):
    return jax.shard_map(
        per_device,
        mesh=mesh,
        in_specs=(P("gx", "gy", "gz"), P("gx", "gy", "gz")),
        out_specs=(P("gx", "gy", "gz"), P("gx", "gy", "gz")),
        check_vma=False,
    )
```

profile of v0, /device:TPU:1, one launch (start us, length us, event | category | flops | bytes accessed | tf_op | source)
XLA Modules:
  0.0 801.9 jit_solution(6088661963511787746)
XLA Ops:
  1.7 8.8 %collective-permute-start = (f32[1,12,512]{2,1,0:T(8,128)S(1)}, f32[1,12,512]{2,1,0:T(8,128)S(1)}, u32[]{:S(2)}, u32[]{:S(2)}) collective-permute-start(f32[1,12,512]{2,1,0:T(8,128)S(1)} %get-tuple-element.128), channel_id=1, source_target_pairs={{64,0},{128,64},{192,128},{256,192},{320,256},{384,320},{448,384},... | collective-permute-start | bytes 73736 | tf_op jit(solution)/shard_map/ppermute | solution.py:24
  79.2 5.8 collective-permute-start.17
  96.1 20.8 %reshape.71 = f32[6,2,6,2,256,2]{5,4,3,2,1,0:T(8,128)} reshape(f32[12,12,512]{2,1,0:T(8,128)S(1)} %get-tuple-element.70) | data formatting | bytes 589824 | tf_op jit(solution)/shard_map/reshape | solution.py:89
  116.8 8.4 %reduce_sum.36 = f32[6,6,256]{2,1,0:T(8,128)} reduce(f32[6,2,6,2,256,2]{5,4,3,2,1,0:T(8,128)} %reshape.71, f32[]{:T(128)} %constant.41.clone.1), dimensions={1,3,5}, to_apply=%region_0.1 | reduce | flops 64512 | bytes 331780 | tf_op jit(solution)/shard_map/reduce_sum | solution.py:90
  187.4 21.6 %reshape.72 = f32[6,2,6,2,256,2]{5,4,3,2,1,0:T(8,128)} reshape(f32[12,12,512]{2,1,0:T(8,128)} %fusion.74) | data formatting | bytes 589824 | tf_op jit(solution)/shard_map/reshape | solution.py:89
  209.0 7.7 reduce_sum.37
  218.2 7.1 collective-permute-start.37
  237.8 6.6 collective-permute-start.41
  322.3 6.4 collective-permute-start.63
  335.9 5.8 collective-permute-start.59
  372.6 6.0 collective-permute-start.71
  477.4 5.8 collective-permute-start.95
  502.6 5.8 collective-permute-start.101
  527.8 5.8 collective-permute-start.107
  562.8 5.8 collective-permute-start.113
  570.6 5.6 collective-permute-start.115
  589.3 5.8 collective-permute-start.119
  612.9 5.8 collective-permute-start.125
  636.6 5.8 collective-permute-start.131
  675.2 5.8 collective-permute-start.137
  708.3 5.8 collective-permute-start.143
  737.4 5.8 collective-permute-start.149
  764.8 5.8 collective-permute-start.155
  791.7 5.9 collective-permute-start.161
  (549 shorter events, 618.2 us)
Async XLA Ops:
  1.7 10.7 %collective-permute-start = (f32[1,12,512]{2,1,0:T(8,128)S(1)}, f32[1,12,512]{2,1,0:T(8,128)S(1)}, u32[]{:S(2)}, u32[]{:S(2)}) collective-permute-start(f32[1,12,512]{2,1,0:T(8,128)S(1)} %get-tuple-element.128), channel_id=1, source_target_pairs={{64,0},{128,64},{192,128},{256,192},{320,256},{384,320},{448,384},... | collective-permute-start | bytes 73736 | tf_op jit(solution)/shard_map/ppermute | solution.py:24
  90.5 34.7 %collective-permute-start.19 = (f32[1,12,512]{2,1,0:T(8,128)}, f32[1,12,512]{2,1,0:T(8,128)}, u32[]{:S(2)}, u32[]{:S(2)}) collective-permute-start(f32[1,12,512]{2,1,0:T(8,128)} %get-tuple-element.122), channel_id=1, source_target_pairs={{0,64},{64,128},{128,192},{192,256},{256,320},{320,384},{384,448},... | collective-permute-start | bytes 73736 | tf_op jit(solution)/shard_map/ppermute | solution.py:23
  94.1 31.1 %collective-permute-start.18 = (f32[1,12,512]{2,1,0:T(8,128)}, f32[1,12,512]{2,1,0:T(8,128)}, u32[]{:S(2)}, u32[]{:S(2)}) collective-permute-start(f32[1,12,512]{2,1,0:T(8,128)} %get-tuple-element.123), channel_id=1, source_target_pairs={{64,0},{128,64},{192,128},{256,192},{320,256},{384,320},{448,384},... | collective-permute-start | bytes 73736 | tf_op jit(solution)/shard_map/ppermute | solution.py:24
  135.1 14.1 %collective-permute-start.22 = (f32[14,14,1]{2,1,0:T(8,128)S(1)}, f32[14,14,1]{2,1,0:T(8,128)S(1)}, u32[]{:S(2)}, u32[]{:S(2)}) collective-permute-start(f32[14,14,1]{2,1,0:T(8,128)S(1)} %get-tuple-element.84), channel_id=1, source_target_pairs={{1,0},{2,1},{3,2},{4,3},{5,4},{6,5},{7,6},{9,8},{10,9},{11,10},{12... | collective-permute-start | bytes 2360 | tf_op jit(solution)/shard_map/ppermute | solution.py:24
  136.4 12.8 %collective-permute-start.23 = (f32[14,14,1]{2,1,0:T(8,128)S(1)}, f32[14,14,1]{2,1,0:T(8,128)S(1)}, u32[]{:S(2)}, u32[]{:S(2)}) collective-permute-start(f32[14,14,1]{2,1,0:T(8,128)S(1)} %get-tuple-element.85), channel_id=1, source_target_pairs={{0,1},{1,2},{2,3},{3,4},{4,5},{5,6},{6,7},{8,9},{9,10},{10,11},{11... | collective-permute-start | bytes 2360 | tf_op jit(solution)/shard_map/ppermute | solution.py:23
  141.9 15.1 %collective-permute-start.24 = (f32[1,6,256]{2,1,0:T(8,128)S(1)}, f32[1,6,256]{2,1,0:T(8,128)S(1)}, u32[]{:S(2)}, u32[]{:S(2)}) collective-permute-start(f32[1,6,256]{2,1,0:T(8,128)S(1)} %get-tuple-element.182), channel_id=1, source_target_pairs={{64,0},{128,64},{192,128},{256,192},{320,256},{384,320},{448,384},... | collective-permute-start | bytes 18440 | tf_op jit(solution)/shard_map/ppermute | solution.py:24
  144.4 12.7 %collective-permute-start.25 = (f32[1,6,256]{2,1,0:T(8,128)S(1)}, f32[1,6,256]{2,1,0:T(8,128)S(1)}, u32[]{:S(2)}, u32[]{:S(2)}) collective-permute-start(f32[1,6,256]{2,1,0:T(8,128)S(1)} %get-tuple-element.183), channel_id=1, source_target_pairs={{0,64},{64,128},{128,192},{192,256},{256,320},{320,384},{384,448},... | collective-permute-start | bytes 18440 | tf_op jit(solution)/shard_map/ppermute | solution.py:23
  171.6 14.3 %collective-permute-start.34 = (f32[14,14,1]{2,1,0:T(8,128)S(1)}, f32[14,14,1]{2,1,0:T(8,128)S(1)}, u32[]{:S(2)}, u32[]{:S(2)}) collective-permute-start(f32[14,14,1]{2,1,0:T(8,128)S(1)} %get-tuple-element.82), channel_id=1, source_target_pairs={{1,0},{2,1},{3,2},{4,3},{5,4},{6,5},{7,6},{9,8},{10,9},{11,10},{12... | collective-permute-start | bytes 2360 | tf_op jit(solution)/shard_map/ppermute | solution.py:24
  172.9 13.0 %collective-permute-start.35 = (f32[14,14,1]{2,1,0:T(8,128)S(1)}, f32[14,14,1]{2,1,0:T(8,128)S(1)}, u32[]{:S(2)}, u32[]{:S(2)}) collective-permute-start(f32[14,14,1]{2,1,0:T(8,128)S(1)} %get-tuple-element.83), channel_id=1, source_target_pairs={{0,1},{1,2},{2,3},{3,4},{4,5},{5,6},{6,7},{8,9},{9,10},{10,11},{11... | collective-permute-start | bytes 2360 | tf_op jit(solution)/shard_map/ppermute | solution.py:23
  178.8 37.8 %collective-permute-start.29 = (f32[8,8,1]{2,1,0:T(8,128)}, f32[8,8,1]{2,1,0:T(8,128)S(1)}, u32[]{:S(2)}, u32[]{:S(2)}) collective-permute-start(f32[8,8,1]{2,1,0:T(8,128)} %get-tuple-element.164), channel_id=1, source_target_pairs={{0,1},{1,2},{2,3},{3,4},{4,5},{5,6},{6,7},{8,9},{9,10},{10,11},{11... | collective-permute-start | bytes 776 | tf_op jit(solution)/shard_map/ppermute | solution.py:23
  184.2 33.2 %collective-permute-start.28 = (f32[8,8,1]{2,1,0:T(8,128)}, f32[8,8,1]{2,1,0:T(8,128)}, u32[]{:S(2)}, u32[]{:S(2)}) collective-permute-start(f32[8,8,1]{2,1,0:T(8,128)} %get-tuple-element.165), channel_id=1, source_target_pairs={{1,0},{2,1},{3,2},{4,3},{5,4},{6,5},{7,6},{9,8},{10,9},{11,10},{12... | collective-permute-start | bytes 776 | tf_op jit(solution)/shard_map/ppermute | solution.py:24
  256.3 13.7 %collective-permute-start.44 = (f32[8,1,256]{2,0,1:T(8,128)}, f32[8,1,256]{2,0,1:T(8,128)}, u32[]{:S(2)}, u32[]{:S(2)}) collective-permute-start(f32[8,1,256]{2,0,1:T(8,128)} %copy.1067), channel_id=1, source_target_pairs={{8,0},{16,8},{24,16},{32,24},{40,32},{48,40},{56,48},{9,1},{17,9},... | collective-permute-start | bytes 24584 | tf_op jit(solution)/shard_map/ppermute | solution.py:24
  258.2 12.6 %collective-permute-start.45 = (f32[8,1,256]{2,0,1:T(8,128)}, f32[8,1,256]{2,0,1:T(8,128)}, u32[]{:S(2)}, u32[]{:S(2)}) collective-permute-start(f32[8,1,256]{2,0,1:T(8,128)} %copy.1069), channel_id=1, source_target_pairs={{0,8},{8,16},{16,24},{24,32},{32,40},{40,48},{48,56},{1,9},{9,17},... | collective-permute-start | bytes 24584 | tf_op jit(solution)/shard_map/ppermute | solution.py:23
  281.0 10.7 %collective-permute-start.49 = (f32[1,6,256]{2,1,0:T(8,128)S(1)}, f32[1,6,256]{2,1,0:T(8,128)S(1)}, u32[]{:S(2)}, u32[]{:S(2)}) collective-permute-start(f32[1,6,256]{2,1,0:T(8,128)S(1)} %get-tuple-element.176), channel_id=1, source_target_pairs={{0,64},{64,128},{128,192},{192,256},{256,320},{320,384},{384,448},... | collective-permute-start | bytes 18440 | tf_op jit(solution)/shard_map/ppermute | solution.py:23
  286.2 11.9 %collective-permute-start.54 = (f32[1,3,128]{2,1,0:T(4,128)S(1)}, f32[1,3,128]{2,1,0:T(4,128)S(1)}, u32[]{:S(2)}, u32[]{:S(2)}) collective-permute-start(f32[1,3,128]{2,1,0:T(4,128)S(1)} %get-tuple-element.232), channel_id=1, source_target_pairs={{64,0},{128,64},{192,128},{256,192},{320,256},{384,320},{448,384},... | collective-permute-start | bytes 4616 | tf_op jit(solution)/shard_map/ppermute | solution.py:24
  298.9 12.2 %collective-permute-start.52 = (f32[8,8,1]{2,1,0:T(8,128)S(1)}, f32[8,8,1]{2,1,0:T(8,128)S(1)}, u32[]{:S(2)}, u32[]{:S(2)}) collective-permute-start(f32[8,8,1]{2,1,0:T(8,128)S(1)} %get-tuple-element.152), channel_id=1, source_target_pairs={{1,0},{2,1},{3,2},{4,3},{5,4},{6,5},{7,6},{9,8},{10,9},{11,10},{12... | collective-permute-start | bytes 776 | tf_op jit(solution)/shard_map/ppermute | solution.py:24
  300.2 10.9 %collective-permute-start.53 = (f32[8,8,1]{2,1,0:T(8,128)S(1)}, f32[8,8,1]{2,1,0:T(8,128)S(1)}, u32[]{:S(2)}, u32[]{:S(2)}) collective-permute-start(f32[8,8,1]{2,1,0:T(8,128)S(1)} %get-tuple-element.153), channel_id=1, source_target_pairs={{0,1},{1,2},{2,3},{3,4},{4,5},{5,6},{6,7},{8,9},{9,10},{10,11},{11... | collective-permute-start | bytes 776 | tf_op jit(solution)/shard_map/ppermute | solution.py:23
  304.9 12.9 %collective-permute-start.57 = (f32[5,1,128]{2,1,0:T(1,128)S(1)}, f32[5,1,128]{2,1,0:T(1,128)S(1)}, u32[]{:S(2)}, u32[]{:S(2)}) collective-permute-start(f32[5,1,128]{2,1,0:T(1,128)S(1)} %get-tuple-element.216), channel_id=1, source_target_pairs={{0,8},{8,16},{16,24},{24,32},{32,40},{40,48},{48,56},{1,9},{9,17},... | collective-permute-start | bytes 7688 | tf_op jit(solution)/shard_map/ppermute | solution.py:23
  329.5 13.4 %collective-permute-start.64 = (f32[8,8,1]{2,1,0:T(8,128)S(1)}, f32[8,8,1]{2,1,0:T(8,128)S(1)}, u32[]{:S(2)}, u32[]{:S(2)}) collective-permute-start(f32[8,8,1]{2,1,0:T(8,128)S(1)} %get-tuple-element.148), channel_id=1, source_target_pairs={{1,0},{2,1},{3,2},{4,3},{5,4},{6,5},{7,6},{9,8},{10,9},{11,10},{12... | collective-permute-start | bytes 776 | tf_op jit(solution)/shard_map/ppermute | solution.py:24
  330.8 12.1 %collective-permute-start.65 = (f32[8,8,1]{2,1,0:T(8,128)S(1)}, f32[8,8,1]{2,1,0:T(8,128)S(1)}, u32[]{:S(2)}, u32[]{:S(2)}) collective-permute-start(f32[8,8,1]{2,1,0:T(8,128)S(1)} %get-tuple-element.149), channel_id=1, source_target_pairs={{0,1},{1,2},{2,3},{3,4},{4,5},{5,6},{6,7},{8,9},{9,10},{10,11},{11... | collective-permute-start | bytes 776 | tf_op jit(solution)/shard_map/ppermute | solution.py:23
  335.9 15.1 %collective-permute-start.59 = (f32[5,5,1]{2,1,0:T(8,128)}, f32[5,5,1]{2,1,0:T(8,128)}, u32[]{:S(2)}, u32[]{:S(2)}) collective-permute-start(f32[5,5,1]{2,1,0:T(8,128)} %get-tuple-element.198), channel_id=1, source_target_pairs={{0,1},{1,2},{2,3},{3,4},{4,5},{5,6},{6,7},{8,9},{9,10},{10,11},{11... | collective-permute-start | bytes 308 | tf_op jit(solution)/shard_map/ppermute | solution.py:23
  540.0 13.8 %collective-permute-start.109 = (f32[1,6,256]{2,1,0:T(8,128)}, f32[1,6,256]{2,1,0:T(8,128)}, u32[]{:S(2)}, u32[]{:S(2)}) collective-permute-start(f32[1,6,256]{2,1,0:T(8,128)} %copy.1092), channel_id=1, source_target_pairs={{0,64},{64,128},{128,192},{192,256},{256,320},{320,384},{384,448},... | collective-permute-start | bytes 18440 | tf_op jit(solution)/shard_map/ppermute | solution.py:23
  646.9 15.7 %collective-permute-start.133 = (f32[1,12,512]{2,1,0:T(8,128)}, f32[1,12,512]{2,1,0:T(8,128)}, u32[]{:S(2)}, u32[]{:S(2)}) collective-permute-start(f32[1,12,512]{2,1,0:T(8,128)} %copy.1126), channel_id=1, source_target_pairs={{0,64},{64,128},{128,192},{192,256},{256,320},{320,384},{384,448},... | collective-permute-start | bytes 73736 | tf_op jit(solution)/shard_map/ppermute | solution.py:23
  651.4 11.3 %collective-permute-start.132 = (f32[1,12,512]{2,1,0:T(8,128)}, f32[1,12,512]{2,1,0:T(8,128)}, u32[]{:S(2)}, u32[]{:S(2)}) collective-permute-start(f32[1,12,512]{2,1,0:T(8,128)} %copy.1123), channel_id=1, source_target_pairs={{64,0},{128,64},{192,128},{256,192},{320,256},{384,320},{448,384},... | collective-permute-start | bytes 73736 | tf_op jit(solution)/shard_map/ppermute | solution.py:24
  (160 other events, 1550.1 us)
where the time goes:
time: 818 us; the launch traced here: 802 us
  starting transfers between devices  495 us (61%)
  waiting for transfers between devices  160 us (20%)
  local copies, waits for them, and re-layouts  84.6 us (10%)
  other arithmetic  59.1 us (7%)
    ppermute x81, starting transfers between devices, with_halo(): before = lax.ppermute(last, axis, up)  365 us
    ppermute x81, waiting for transfers between devices, with_halo(): after = lax.ppermute(leading, axis, down)  130 us
    ppermute x81, starting transfers between devices, with_halo(): after = lax.ppermute(leading, axis, down)  129 us
    reshape x3, local copies, waits for them, and re-layouts, restrict(): values.reshape(sizes[0] // 2, 2, sizes[1] // 2, 2, sizes[2] // 2, 2)  47 us
    ppermute x81, waiting for transfers between devices, with_halo(): before = lax.ppermute(last, axis, up)  29.7 us
    reduce_sum x4, other arithmetic, restrict(): return jnp.mean(grouped, axis=(1, 3, 5))  21.1 us
    broadcast_in_dim x26, local copies, waits for them, and re-layouts, prolong(): return jnp.repeat(jnp.repeat(jnp.repeat(values, 2, 0), 2, 1), 2, 2)  18.5 us
  transfers between devices with their start and end apart: 162, of which 73 were waited for; matrix products, arithmetic and copies ran while one was open for 13% of the time, Pallas kernels for 0%

commit v1 on v0

v1 whole, which is shorter than its diff:
```python
import functools

import jax
import jax.numpy as jnp
from jax import lax
from jax.experimental import pallas as pl
from jax.experimental.pallas import tpu as pltpu
from jax.sharding import PartitionSpec as P

MESH = pl.DeviceIdType.MESH
DEGREE = 4
COARSE_ITERS = 8
HEAVY = 20.0
SMOOTH_LOWEST = 0.3
COARSE_LOWEST = 0.02
UPPER = 2.0

LEVELS = (
    dict(n=12, h=6, t=5, cols=24, rows=32),
    dict(n=6, h=8, t=3, cols=22, rows=32),
    dict(n=3, h=8, t=2, cols=19, rows=32),
)


def weights(lowest, degree):
    middle, radius = (UPPER + lowest) / 2.0, (UPPER - lowest) / 2.0
    sharpness = middle / radius
    old = 1.0 / sharpness
    pairs = []
    for _ in range(1, degree):
        new = 1.0 / (2.0 * sharpness - old)
        pairs.append((new * old, 2.0 * new / radius))
        old = new
    return 1.0 / middle, pairs


def columns(lo, hi, unroll, body, carry):
    trips = (hi - lo) // unroll

    def several(k, c):
        for j in range(unroll):
            c = body(lo + k * unroll + j, c)
        return c

    if trips > 1:
        carry = lax.fori_loop(0, trips, several, carry)
    elif trips == 1:
        carry = several(0, carry)
    for i in range(lo + trips * unroll, hi):
        carry = body(i, carry)
    return carry


def lanes(shape):
    return lax.broadcasted_iota(jnp.int32, shape, len(shape) - 1)


def shifted(blocks, towards):
    count = len(blocks)
    shape = blocks[0].shape
    edge = lanes(shape) == (127 if towards > 0 else 0)
    rolled = [pltpu.roll(v, 127 if towards > 0 else 1, 1) for v in blocks]
    return [jnp.where(edge, rolled[(t + towards) % count], rolled[t]) for t in range(count)]


def split(block):
    return [block[t] for t in range(block.shape[0])]


def picked(value, index):
    return jnp.take_along_axis(value, index, axis=1)


def halved(blocks):
    lane = lanes(blocks[0].shape)
    index = (2 * lane) % 128
    pairs = [picked(v + pltpu.roll(v, 127, 1), index) for v in blocks]
    out = [jnp.where(lane < 64, pairs[2 * t], pairs[2 * t + 1]) for t in range(len(blocks) // 2)]
    out.append(pairs[-1])
    return out


def doubled(blocks):
    lane = lanes(blocks[0].shape)
    low, high = lane // 2, 64 + lane // 2
    out = []
    for v in blocks[:-1]:
        out += [picked(v, low), picked(v, high)]
    out.append(picked(blocks[-1], jnp.where(lane < 64, low, high)))
    return out


def reach(offset, n, w):
    return max(offset * n, -w), min(offset * n + n, n + w)


class Sender:
    def __init__(self, send_sems, recv_sems, sizes):
        self.send, self.recv, self.used = send_sems, recv_sems, 0
        self.sizes = sizes
        self.pending = []

    def target(self, offset):
        place = []
        for axis, o in zip(("gx", "gy", "gz"), offset):
            size = self.sizes[axis]
            place.append(lax.rem(lax.axis_index(axis) + (o + 4 * size), size) if o else lax.axis_index(axis))
        return tuple(place)

    def start(self, src, dst, offset):
        copy = pltpu.make_async_remote_copy(
            src_ref=src,
            dst_ref=dst,
            send_sem=self.send.at[self.used],
            recv_sem=self.recv.at[self.used],
            device_id=self.target(offset),
            device_id_type=MESH,
        )
        copy.start()
        self.used += 1
        return copy

    def exchange(self, ref, level, w, offsets, tiles=None, whole_y=False):
        n, h = level["n"], level["h"]
        t0, t1 = tiles or (0, level["t"])
        copies = []
        for ox, oy in offsets:
            x0, x1 = reach(ox, n, w)
            if whole_y:
                y0, y1 = -w, n + w
            else:
                y0, y1 = reach(oy, n, w)
            sx, sy = x0 - ox * n + h, y0 - oy * n + h
            copies.append(
                self.start(
                    ref.at[sx : sx + x1 - x0, t0:t1, sy : sy + y1 - y0, :],
                    ref.at[x0 + h : x1 + h, t0:t1, y0 + h : y1 + h, :],
                    (-ox, -oy, 0),
                )
            )
        return copies


def wait_recv(copies):
    for copy in copies:
        copy.wait_recv()


def wait_send(copies):
    for copy in copies:
        copy.wait_send()


def near(o, n):
    return (abs(o) - 1) * n + 1 if o else 0


def diamond(n, w, most):
    found = []
    for ox in range(-most, most + 1):
        for oy in range(-most, most + 1):
            if (ox or oy) and near(ox, n) + near(oy, n) <= w:
                found.append((ox, oy))
    return sorted(found, key=lambda o: -abs(o[0]) - abs(o[1]))


AROUND = diamond(1, 2, 1)


def clear_outside(ref, level, w, sizes):
    n, h, t = level["n"], level["h"], level["t"]

    def clear(x0, x1, y0, y1):
        zero = jnp.zeros((t, y1 - y0, 128), jnp.float32)

        def body(i, c):
            ref[i, :, y0:y1, :] = zero
            return c

        lax.fori_loop(x0, x1, body, 0)

    gx, gy = lax.axis_index("gx"), lax.axis_index("gy")
    for k in range(-(-w // n)):
        below, above = (h - w, h - k * n), (h + n + k * n, h + n + w)
        every = (h - w, h + n + w)
        pl.when(gx == k)(functools.partial(clear, *below, *every))
        pl.when(gx == sizes["gx"] - 1 - k)(functools.partial(clear, *above, *every))
        pl.when(gy == k)(functools.partial(clear, *every, *below))
        pl.when(gy == sizes["gy"] - 1 - k)(functools.partial(clear, *every, *above))


def conduct(a, b, scale):
    return scale / jnp.maximum(a + b, 0.5)


def coefficients(rho, co, level, w, scale, unroll, first=None):
    bx, by, bzp, bzm, iv = co
    n, h = level["n"], level["h"]
    lo, hi, rows = h - w, h + n + w, n + 2 * w
    ys = pl.ds(lo, rows)

    def body(i, before):
        here = rho[i, :, ys, :]
        after = conduct(here, rho[i + 1, :, ys, :], scale)
        bx[i, :, ys, :] = after
        by[i, :, pl.ds(lo - 1, rows + 1), :] = conduct(
            rho[i, :, pl.ds(lo - 1, rows + 1), :], rho[i, :, pl.ds(lo, rows + 1), :], scale
        )
        above = jnp.stack([conduct(a, b, scale) for a, b in zip(split(here), shifted(split(here), 1))])
        below = jnp.stack(shifted(split(above), -1))
        bzp[i, :, ys, :] = above
        bzm[i, :, ys, :] = below
        total = (before + after) + (above + below) + (by[i, :, ys, :] + by[i, :, pl.ds(lo - 1, rows), :])
        inverse = jnp.where(here > 0.0, 1.0 / total, 0.0)
        iv[i, :, ys, :] = inverse
        if first is not None:
            r, d, weight = first
            d[i, :, ys, :] = weight * (inverse * r[i, :, ys, :])
        return after

    start = conduct(rho[lo - 1, :, ys, :], rho[lo, :, ys, :], scale)
    bx[lo - 1, :, ys, :] = start
    columns(lo, hi, unroll, body, start)


def begin(r, iv, d, level, w, weight, unroll):
    n, h = level["n"], level["h"]
    ys = pl.ds(h - w, n + 2 * w)

    def body(i, c):
        d[i, :, ys, :] = weight * (iv[i, :, ys, :] * r[i, :, ys, :])
        return c

    columns(h - w, h + n + w, unroll, body, 0)


def sweep(v, co, level, w, unroll, finish, tiles=None):
    bx, by, bzp, bzm, _ = co
    n, h, t = level["n"], level["h"], level["t"]
    lo, hi, rows = h - w, h + n + w, n + 2 * w
    ys, up, down = pl.ds(lo, rows), pl.ds(lo + 1, rows), pl.ds(lo - 1, rows)

    def body(i, carry):
        here, before = carry
        after = v[i + 1, :, ys, :]
        flux = bx[i, :, ys, :] * (here - after)
        parts = split(here)
        zp = jnp.stack(shifted(parts, 1))
        zm = jnp.stack(shifted(parts, -1))
        total = (flux - before) + bzp[i, :, ys, :] * (here - zp) + bzm[i, :, ys, :] * (here - zm)
        total = total + by[i, :, ys, :] * (here - v[i, :, up, :])
        total = total + by[i, :, down, :] * (here - v[i, :, down, :])
        finish(i, ys, here, total)
        return after, flux

    here = v[lo, :, ys, :]
    before = bx[lo - 1, :, ys, :] * (v[lo - 1, :, ys, :] - here)
    columns(lo, hi, unroll, body, (here, before))


def smooth(v, r, d, co, level, w, alpha, beta, unroll, total=None):
    iv = co[4]

    def finish(i, ys, here, applied):
        rest = r[i, :, ys, :] - applied
        r[i, :, ys, :] = rest
        new = beta * (iv[i, :, ys, :] * rest)
        if alpha is not None:
            new = alpha * here + new
        d[i, :, ys, :] = new
        if total is not None:
            total[i, :, ys, :] = total[i, :, ys, :] + new

    sweep(v, co, level, w, unroll, finish)


def restricted(fine, coarse, level_fine, level_coarse):
    h, n, hc = level_fine["h"], level_coarse["n"], level_coarse["h"]

    def body(i, c):
        x = h + 2 * i
        even, odd = pl.ds(h, n, stride=2), pl.ds(h + 1, n, stride=2)
        blocks = []
        for t in range(level_fine["t"]):
            both = fine[x, t, even, :] + fine[x, t, odd, :]
            both = both + (fine[x + 1, t, even, :] + fine[x + 1, t, odd, :])
            blocks.append(both)
        coarse[hc + i, :, hc : hc + n, :] = jnp.stack(halved(blocks)) * 0.125
        return c

    for i in range(n):
        body(i, 0)


def prolonged(coarse, fine, level_coarse, level_fine, w):
    hc, h, n = level_coarse["h"], level_fine["h"], level_coarse["n"]
    count = n + 2 * w

    def body(k, c):
        block = doubled(split(coarse[hc - w + k, :, hc - w : hc - w + count, :]))
        for t, v in enumerate(block):
            for x in (0, 1):
                for y in (0, 1):
                    fine[h - 2 * w + 2 * k + x, t, pl.ds(h - 2 * w + y, count, stride=2), :] = v
        return c

    columns(0, count, 3, body, 0)


def kernel(sizes, rhs, phase, out_x, out_r, *scratch):
    scratch = list(scratch)

    def take(count):
        taken, scratch[:count] = scratch[:count], []
        return taken

    rho0, r0, up0, u0, x0, d01, d02, d03, d04 = take(9)
    co0 = take(5)
    rho1, r1, up1, u1, x1, d11, d12, d13, d14 = take(9)
    co1 = take(5)
    rho2, r2, x2, d21, d22 = take(5)
    co2 = take(5)
    zs_up, zs_down, zr_below, zr_above, send_sems, recv_sems = take(6)
    l0, l1, l2 = LEVELS
    sender = Sender(send_sems, recv_sems, sizes)
    first, pairs = weights(SMOOTH_LOWEST, DEGREE)
    first2, pairs2 = weights(COARSE_LOWEST, COARSE_ITERS)

    coarse_offsets = diamond(3, 7, 3)
    line = [(o, 0) for o in (3, -3, 2, -2)] + [(0, o) for o in (3, -3, 2, -2)]
    met = {(ox, oy, 0) for ox, oy in coarse_offsets + line + AROUND} | {(0, 0, 1), (0, 0, -1)}
    barrier = pltpu.get_barrier_semaphore()
    for offset in sorted(met):
        pl.semaphore_signal(barrier, inc=1, device_id=sender.target(offset), device_id_type=MESH)

    lane = lanes((12, 128))
    own = slice(l0["h"], l0["h"] + 12)

    def prepare(i, c):
        blocks = []
        for t in range(4):
            part = slice(128 * t, 128 * t + 128)
            value = rhs[i, :, part]
            density = jnp.where(phase[i, :, part] == 1, HEAVY, 1.0).astype(jnp.float32)
            r0[i + l0["h"], t, own, :] = value
            rho0[i + l0["h"], t, own, :] = density
            blocks.append((value, density))
        zs_up[i, :12, :] = jnp.where(lane >= 64, blocks[3][0], pltpu.roll(blocks[3][1], 64, 1))
        zs_down[i, :12, :] = jnp.where(lane < 64, blocks[0][0], pltpu.roll(blocks[0][1], 64, 1))
        return c

    columns(0, 12, 4, prepare, 0)
    pl.semaphore_wait(barrier, len(met))

    along_z = [
        sender.start(zs_up.at[:, :12, :], zr_below.at[:, :12, :], (0, 0, 1)),
        sender.start(zs_down.at[:, :12, :], zr_above.at[:, :12, :], (0, 0, -1)),
    ]
    fine = sender.exchange(rho0, l0, 5, AROUND, (0, 4))
    fine += sender.exchange(r0, l0, 4, AROUND, (0, 4))

    wait_recv(along_z)
    gz = lax.axis_index("gz")
    inside = jnp.where(lane < 64, jnp.where(gz == sizes["gz"] - 1, 0.0, 1.0), jnp.where(gz == 0, 0.0, 1.0))

    def ends(i, c):
        below, above = zr_below[i, :12, :], zr_above[i, :12, :]
        r0[i + l0["h"], 4, own, :] = jnp.where(lane < 64, above, below)
        rho0[i + l0["h"], 4, own, :] = inside * pltpu.roll(jnp.where(lane < 64, below, above), 64, 1)
        return c

    columns(0, 12, 6, ends, 0)
    fine += sender.exchange(rho0, l0, 5, AROUND, (4, 5))
    fine += sender.exchange(r0, l0, 4, AROUND, (4, 5))

    restricted(rho0, rho1, l0, l1)
    restricted(rho1, rho2, l1, l2)
    line_y1, line_y2 = [(0, o) for o in (2, -2, 1, -1)], [(0, o) for o in (3, -3, 2, -2, 1, -1)]
    line_x1, line_x2 = [(o, 0) for _, o in line_y1], [(o, 0) for _, o in line_y2]
    density_y = sender.exchange(rho1, l1, 7, line_y1) + sender.exchange(rho2, l2, 8, line_y2)

    wait_recv(fine)
    wait_send(fine)
    clear_outside(rho0, l0, 5, sizes)
    coefficients(rho0, co0, l0, 4, 2.0, 1, (r0, d01, first))
    wait_recv(density_y)
    density_x = sender.exchange(rho1, l1, 7, line_x1, whole_y=True)
    density_x += sender.exchange(rho2, l2, 8, line_x2, whole_y=True)
    smooth(d01, r0, d02, co0, l0, 3, *pairs[0], 3)
    smooth(d02, r0, d03, co0, l0, 2, *pairs[1], 4)
    smooth(d03, r0, d04, co0, l0, 1, *pairs[2], 4)

    def finish_down0(i, ys, here, applied):
        up0[i, :, ys, :] = r0[i, :, ys, :] - applied
        x0[i, :, ys, :] = (d01[i, :, ys, :] + d02[i, :, ys, :]) + (d03[i, :, ys, :] + here)

    sweep(d04, co0, l0, 0, 4, finish_down0)

    restricted(up0, r1, l0, l1)
    second = sender.exchange(r1, l1, 4, AROUND)
    back0 = sender.exchange(up0, l0, 4, AROUND)
    wait_recv(density_x)
    wait_send(density_y)
    wait_send(density_x)
    clear_outside(rho1, l1, 7, sizes)
    clear_outside(rho2, l2, 8, sizes)
    coefficients(rho1, co1, l1, 6, 0.5, 2)
    coefficients(rho2, co2, l2, 7, 0.125, 2)
    wait_recv(second)
    wait_send(second)
    begin(r1, co1[4], d11, l1, 4, first, 7)
    smooth(d11, r1, d12, co1, l1, 3, *pairs[0], 6)
    smooth(d12, r1, d13, co1, l1, 2, *pairs[1], 5)
    smooth(d13, r1, d14, co1, l1, 1, *pairs[2], 8)

    def finish_down1(i, ys, here, applied):
        up1[i, :, ys, :] = r1[i, :, ys, :] - applied
        x1[i, :, ys, :] = (d11[i, :, ys, :] + d12[i, :, ys, :]) + (d13[i, :, ys, :] + here)

    sweep(d14, co1, l1, 0, 6, finish_down1)

    restricted(up1, r2, l1, l2)
    third = sender.exchange(r2, l2, 7, coarse_offsets)
    back1 = sender.exchange(up1, l1, 6, AROUND) + sender.exchange(x1, l1, 3, AROUND)
    wait_recv(third)
    wait_send(third)
    begin(r2, co2[4], d21, l2, 7, first2, 17)

    def copy_total(i, c):
        x2[i, :, l2["h"] : l2["h"] + 3, :] = d21[i, :, l2["h"] : l2["h"] + 3, :]
        return c

    columns(l2["h"], l2["h"] + 3, 3, copy_total, 0)
    v, d = d21, d22
    for k, (alpha, beta) in enumerate(pairs2):
        smooth(v, r2, d, co2, l2, 6 - k, alpha, beta, 8)
        v, d = d, v

        def add_total(i, c, v=v):
            x2[i, :, l2["h"] : l2["h"] + 3, :] = x2[i, :, l2["h"] : l2["h"] + 3, :] + v[i, :, l2["h"] : l2["h"] + 3, :]
            return c

        columns(l2["h"], l2["h"] + 3, 3, add_total, 0)

    fourth = sender.exchange(x2, l2, 4, diamond(3, 4, 2))
    wait_recv(back1)
    wait_send(back1)
    wait_recv(fourth)
    clear_outside(x2, l2, 4, sizes)
    prolonged(x2, u1, l2, l1, 4)
    smooth(u1, up1, d11, co1, l1, 6, None, first, 6)
    smooth(d11, up1, d12, co1, l1, 5, *pairs[0], 8)
    smooth(d12, up1, d13, co1, l1, 4, *pairs[1], 7)
    smooth(d13, up1, d14, co1, l1, 3, *pairs[2], 6)
    reach1 = pl.ds(l1["h"] - 3, 12)

    def finish_up1(i, c):
        total = (x1[i, :, reach1, :] + u1[i, :, reach1, :]) + (d11[i, :, reach1, :] + d12[i, :, reach1, :])
        x1[i, :, reach1, :] = total + (d13[i, :, reach1, :] + d14[i, :, reach1, :])
        return c

    columns(l1["h"] - 3, l1["h"] + 9, 6, finish_up1, 0)
    clear_outside(x1, l1, 3, sizes)

    prolonged(x1, u0, l1, l0, 3)
    wait_recv(back0)
    wait_send(back0)
    smooth(u0, up0, d01, co0, l0, 4, None, first, 3)
    smooth(d01, up0, d02, co0, l0, 3, *pairs[0], 3)
    smooth(d02, up0, d03, co0, l0, 2, *pairs[1], 4)
    smooth(d03, up0, d04, co0, l0, 1, *pairs[2], 4)

    def finish_up0(i, ys, here, applied):
        j = i - l0["h"]
        total = (x0[i, :, ys, :] + u0[i, :, ys, :]) + (d01[i, :, ys, :] + d02[i, :, ys, :])
        total = total + (d03[i, :, ys, :] + here)
        rest = up0[i, :, ys, :] - applied
        for t in range(4):
            out_x[j, :, 128 * t : 128 * t + 128] = total[t]
            out_r[j, :, 128 * t : 128 * t + 128] = rest[t]

    sweep(d04, co0, l0, 0, 4, finish_up0)
    wait_send(along_z)
    wait_send(fourth)


COPIES = 2 + 32 + 20 + 8 + 8 + 24 + 16 + 12


def per_device(sizes, right_side, phase):
    def field(level):
        return pltpu.VMEM((level["cols"], level["t"], level["rows"], 128), jnp.float32)

    l0, l1, l2 = LEVELS
    shape = jax.ShapeDtypeStruct(right_side.shape, jnp.float32)
    whole = pl.BlockSpec(memory_space=pltpu.VMEM)
    return pl.pallas_call(
        functools.partial(kernel, sizes),
        out_shape=(shape, shape),
        in_specs=[whole, whole],
        out_specs=(whole, whole),
        scratch_shapes=[field(l0)] * 14
        + [field(l1)] * 14
        + [field(l2)] * 10
        + [pltpu.VMEM((12, 16, 128), jnp.float32)] * 4
        + [pltpu.SemaphoreType.DMA((COPIES,))] * 2,
        compiler_params=pltpu.CompilerParams(
            collective_id=0, has_side_effects=True, vmem_limit_bytes=56 * 1024 * 1024
        ),
        cost_estimate=pl.CostEstimate(flops=60_000_000, bytes_accessed=1_200_000, transcendentals=0),
        name="cycle",
    )(right_side, phase)


def solution(mesh):
    spec = P("gx", "gy", "gz")
    return jax.shard_map(
        functools.partial(per_device, dict(mesh.shape)),
        mesh=mesh,
        in_specs=(spec, spec),
        out_specs=(spec, spec),
        check_vma=False,
    )
```

time: 818 us -> 70.5 us (0.09); the launches traced: 802 us -> 70.3 us
  starting transfers between devices: 495 us -> 0 us
  waiting for transfers between devices: 160 us -> 0 us
  local copies, waits for them, and re-layouts: 84.6 us -> 2.57 us
  Pallas kernels: 0 us -> 67.1 us
  other arithmetic: 59.1 us -> 0 us
    ppermute x162 -> x0, starting transfers between devices: 495 us -> none  [the longest x81 365 us: with_halo(): before = lax.ppermute(last, axis, up)]
    ppermute x162 -> x0, waiting for transfers between devices: 160 us -> none  [the longest x81 130 us: with_halo(): after = lax.ppermute(leading, axis, down)]
    pallas_call x0 -> x1, Pallas kernels: none -> 67.1 us  [per_device(): pl.pallas_call(functools.partial(kernel, sizes), out_shape=(shape, shape)...]
    reshape x9 -> x0, local copies, waits for them, and re-layouts: 53.6 us -> none  [the longest x3 47 us: restrict(): values.reshape(sizes[0] // 2, 2, sizes[1] // 2, 2, sizes[2] // 2, 2)]
    reduce_sum x4 -> x0, other arithmetic: 21.1 us -> none  [restrict(): return jnp.mean(grouped, axis=(1, 3, 5))]
    broadcast_in_dim x26 -> x0, local copies, waits for them, and re-layouts: 18.5 us -> none  [prolong(): return jnp.repeat(jnp.repeat(jnp.repeat(values, 2, 0), 2, 1), 2, 2)]
    add x20 -> x0, other arithmetic: 17.8 us -> none  [the longest x17 15.6 us: chebyshev(): weight_new * weight_old * direction]
  transfers between devices with their start and end apart: 162 -> 0, of which waited for: 73 -> 0; matrix products, arithmetic and copies ran while one was open for 13% -> 0% of each run, Pallas kernels for 0% -> 0%
where the time goes in v1:
time: 70.5 us; the launch traced here: 70.3 us
  Pallas kernels  67.1 us (95%)
  local copies, waits for them, and re-layouts  2.57 us (4%)
    pallas_call x1, Pallas kernels, per_device(): pl.pallas_call(functools.partial(kernel, sizes), out_shape=(shape, shape)...  67.1 us
    unnamed x4, local copies, waits for them, and re-layouts  2.57 us

profile of v1, /device:TPU:1, one launch (start us, length us, event | category | flops | bytes accessed | tf_op | source)
XLA Modules:
  0.0 70.3 jit_solution(3384192015556049678)
XLA Ops:
  0.6 67.1 %cycle.1 = (f32[12,12,512]{2,1,0:T(8,128)}, f32[12,12,512]{2,1,0:T(8,128)}) custom-call(f32[12,12,512]{2,1,0:T(8,128)} %rhs.1, s32[12,12,512]{2,1,0:T(8,128)} %phase.1), custom_call_target="tpu_custom_call" | custom-call | flops 60000000 | bytes 1200000 | tf_op jit(solution)/shard_map/cycle/pallas_call | solution.py:497
  67.8 0.0 copy-start
  67.8 1.8 %copy.6 = f32[12,12,512]{2,1,0:T(8,128)} copy(f32[12,12,512]{2,1,0:T(8,128)} %get-tuple-element.4) | data formatting | bytes 589824
  69.6 0.0 copy-done
  69.6 0.7 %copy.7 = f32[12,12,512]{2,1,0:T(8,128)} copy(f32[12,12,512]{2,1,0:T(8,128)S(1)} %copy-done) | data formatting | bytes 589824
Async XLA Ops:
  67.8 1.8 %copy-start = (f32[12,12,512]{2,1,0:T(8,128)S(1)}, f32[12,12,512]{2,1,0:T(8,128)}, u32[]{:S(2)}) copy-start(f32[12,12,512]{2,1,0:T(8,128)} %get-tuple-element.5) | copy-start | bytes 884740

commit v2 on v1

--- a/solution.py
+++ b/solution.py
@@ -88,6 +88,10 @@
         out += [picked(v, low), picked(v, high)]
     out.append(picked(blocks[-1], jnp.where(lane < 64, low, high)))
     return out
+
+
+def near(o, n):
+    return (abs(o) - 1) * n + 1 if o else 0
 
 
 def reach(offset, n, w):
@@ -125,11 +129,8 @@
         t0, t1 = tiles or (0, level["t"])
         copies = []
         for ox, oy in offsets:
-            x0, x1 = reach(ox, n, w)
-            if whole_y:
-                y0, y1 = -w, n + w
-            else:
-                y0, y1 = reach(oy, n, w)
+            x0, x1 = reach(ox, n, w - near(oy, n))
+            y0, y1 = (-w, n + w) if whole_y else reach(oy, n, w - near(ox, n))
             sx, sy = x0 - ox * n + h, y0 - oy * n + h
             copies.append(
                 self.start(
@@ -151,10 +152,6 @@
         copy.wait_send()
 
 
-def near(o, n):
-    return (abs(o) - 1) * n + 1 if o else 0
-
-
 def diamond(n, w, most):
     found = []
     for ox in range(-most, most + 1):
@@ -193,7 +190,7 @@
     return scale / jnp.maximum(a + b, 0.5)
 
 
-def coefficients(rho, co, level, w, scale, unroll, first=None):
+def coefficients(rho, co, level, w, scale, unroll):
     bx, by, bzp, bzm, iv = co
     n, h = level["n"], level["h"]
     lo, hi, rows = h - w, h + n + w, n + 2 * w
@@ -213,9 +210,6 @@
         total = (before + after) + (above + below) + (by[i, :, ys, :] + by[i, :, pl.ds(lo - 1, rows), :])
         inverse = jnp.where(here > 0.0, 1.0 / total, 0.0)
         iv[i, :, ys, :] = inverse
-        if first is not None:
-            r, d, weight = first
-            d[i, :, ys, :] = weight * (inverse * r[i, :, ys, :])
         return after
 
     start = conduct(rho[lo - 1, :, ys, :], rho[lo, :, ys, :], scale)
@@ -320,33 +314,42 @@
     co1 = take(5)
     rho2, r2, x2, d21, d22 = take(5)
     co2 = take(5)
-    zs_up, zs_down, zr_below, zr_above, send_sems, recv_sems = take(6)
+    kind, zs_up, zs_down, zr_below, zr_above, local_sems, send_sems, recv_sems = take(8)
     l0, l1, l2 = LEVELS
     sender = Sender(send_sems, recv_sems, sizes)
     first, pairs = weights(SMOOTH_LOWEST, DEGREE)
     first2, pairs2 = weights(COARSE_LOWEST, COARSE_ITERS)
+    own = slice(l0["h"], l0["h"] + 12)
+
+    loads = [pltpu.make_async_copy(phase, kind, local_sems.at[4])]
+    for t in range(4):
+        loads.append(
+            pltpu.make_async_copy(rhs.at[:, :, 128 * t : 128 * t + 128], r0.at[own, t, own, :], local_sems.at[t])
+        )
+    for copy in loads:
+        copy.start()
 
     coarse_offsets = diamond(3, 7, 3)
-    line = [(o, 0) for o in (3, -3, 2, -2)] + [(0, o) for o in (3, -3, 2, -2)]
-    met = {(ox, oy, 0) for ox, oy in coarse_offsets + line + AROUND} | {(0, 0, 1), (0, 0, -1)}
+    line_y2 = [(0, o) for o in (3, -3, 2, -2, 1, -1)]
+    line_x2 = [(o, 0) for _, o in line_y2]
+    met = {(ox, oy, 0) for ox, oy in coarse_offsets + line_y2 + line_x2 + AROUND} | {(0, 0, 1), (0, 0, -1)}
     barrier = pltpu.get_barrier_semaphore()
     for offset in sorted(met):
         pl.semaphore_signal(barrier, inc=1, device_id=sender.target(offset), device_id_type=MESH)
 
     lane = lanes((12, 128))
-    own = slice(l0["h"], l0["h"] + 12)
+    for copy in loads:
+        copy.wait()
 
     def prepare(i, c):
-        blocks = []
+        x = i + l0["h"]
+        density = []
         for t in range(4):
             part = slice(128 * t, 128 * t + 128)
-            value = rhs[i, :, part]
-            density = jnp.where(phase[i, :, part] == 1, HEAVY, 1.0).astype(jnp.float32)
-            r0[i + l0["h"], t, own, :] = value
-            rho0[i + l0["h"], t, own, :] = density
-            blocks.append((value, density))
-        zs_up[i, :12, :] = jnp.where(lane >= 64, blocks[3][0], pltpu.roll(blocks[3][1], 64, 1))
-        zs_down[i, :12, :] = jnp.where(lane < 64, blocks[0][0], pltpu.roll(blocks[0][1], 64, 1))
+            density.append(jnp.where(kind[i, :, part] == 1, HEAVY, 1.0).astype(jnp.float32))
+            rho0[x, t, own, :] = density[t]
+        zs_up[i, :12, :] = jnp.where(lane >= 64, r0[x, 3, own, :], pltpu.roll(density[3], 64, 1))
+        zs_down[i, :12, :] = jnp.where(lane < 64, r0[x, 0, own, :], pltpu.roll(density[0], 64, 1))
         return c
 
     columns(0, 12, 4, prepare, 0)
@@ -356,8 +359,7 @@
         sender.start(zs_up.at[:, :12, :], zr_below.at[:, :12, :], (0, 0, 1)),
         sender.start(zs_down.at[:, :12, :], zr_above.at[:, :12, :], (0, 0, -1)),
     ]
-    fine = sender.exchange(rho0, l0, 5, AROUND, (0, 4))
-    fine += sender.exchange(r0, l0, 4, AROUND, (0, 4))
+    fine_rho = sender.exchange(rho0, l0, 5, AROUND, (0, 4))
 
     wait_recv(along_z)
     gz = lax.axis_index("gz")
@@ -370,22 +372,21 @@
         return c
 
     columns(0, 12, 6, ends, 0)
-    fine += sender.exchange(rho0, l0, 5, AROUND, (4, 5))
-    fine += sender.exchange(r0, l0, 4, AROUND, (4, 5))
+    fine_rho += sender.exchange(rho0, l0, 5, AROUND, (4, 5))
+    fine_r = sender.exchange(r0, l0, 4, AROUND)
 
     restricted(rho0, rho1, l0, l1)
     restricted(rho1, rho2, l1, l2)
-    line_y1, line_y2 = [(0, o) for o in (2, -2, 1, -1)], [(0, o) for o in (3, -3, 2, -2, 1, -1)]
-    line_x1, line_x2 = [(o, 0) for _, o in line_y1], [(o, 0) for _, o in line_y2]
-    density_y = sender.exchange(rho1, l1, 7, line_y1) + sender.exchange(rho2, l2, 8, line_y2)
-
-    wait_recv(fine)
-    wait_send(fine)
+    density1 = sender.exchange(rho1, l1, 7, diamond(6, 7, 2))
+    density2 = sender.exchange(rho2, l2, 8, line_y2)
+
+    wait_recv(fine_rho)
+    wait_send(fine_rho)
     clear_outside(rho0, l0, 5, sizes)
-    coefficients(rho0, co0, l0, 4, 2.0, 1, (r0, d01, first))
-    wait_recv(density_y)
-    density_x = sender.exchange(rho1, l1, 7, line_x1, whole_y=True)
-    density_x += sender.exchange(rho2, l2, 8, line_x2, whole_y=True)
+    coefficients(rho0, co0, l0, 4, 2.0, 1)
+    wait_recv(fine_r)
+    wait_send(fine_r)
+    begin(r0, co0[4], d01, l0, 4, first, 4)
     smooth(d01, r0, d02, co0, l0, 3, *pairs[0], 3)
     smooth(d02, r0, d03, co0, l0, 2, *pairs[1], 4)
     smooth(d03, r0, d04, co0, l0, 1, *pairs[2], 4)
@@ -398,14 +399,13 @@
 
     restricted(up0, r1, l0, l1)
     second = sender.exchange(r1, l1, 4, AROUND)
+    wait_recv(density2)
+    density2x = sender.exchange(rho2, l2, 8, line_x2, whole_y=True)
     back0 = sender.exchange(up0, l0, 4, AROUND)
-    wait_recv(density_x)
-    wait_send(density_y)
-    wait_send(density_x)
+    wait_recv(density1)
+    wait_send(density1)
     clear_outside(rho1, l1, 7, sizes)
-    clear_outside(rho2, l2, 8, sizes)
     coefficients(rho1, co1, l1, 6, 0.5, 2)
-    coefficients(rho2, co2, l2, 7, 0.125, 2)
     wait_recv(second)
     wait_send(second)
     begin(r1, co1[4], d11, l1, 4, first, 7)
@@ -422,6 +422,10 @@
     restricted(up1, r2, l1, l2)
     third = sender.exchange(r2, l2, 7, coarse_offsets)
     back1 = sender.exchange(up1, l1, 6, AROUND) + sender.exchange(x1, l1, 3, AROUND)
+    wait_recv(density2x)
+    wait_send(density2 + density2x)
+    clear_outside(rho2, l2, 8, sizes)
+    coefficients(rho2, co2, l2, 7, 0.125, 2)
     wait_recv(third)
     wait_send(third)
     begin(r2, co2[4], d21, l2, 7, first2, 17)
@@ -484,7 +488,7 @@
     wait_send(fourth)
 
 
-COPIES = 2 + 32 + 20 + 8 + 8 + 24 + 16 + 12
+COPIES = 2 + 24 + 12 + 12 + 8 + 6 + 8 + 24 + 16 + 12
 
 
 def per_device(sizes, right_side, phase):
@@ -492,17 +496,20 @@
         return pltpu.VMEM((level["cols"], level["t"], level["rows"], 128), jnp.float32)
 
     l0, l1, l2 = LEVELS
-    shape = jax.ShapeDtypeStruct(right_side.shape, jnp.float32)
+    shape = right_side.shape
+    result = pltpu.VMEM(shape, jnp.float32)
     whole = pl.BlockSpec(memory_space=pltpu.VMEM)
     return pl.pallas_call(
         functools.partial(kernel, sizes),
-        out_shape=(shape, shape),
-        in_specs=[whole, whole],
+        out_shape=(result, result),
+        in_specs=[pl.BlockSpec(memory_space=pl.ANY)] * 2,
         out_specs=(whole, whole),
         scratch_shapes=[field(l0)] * 14
         + [field(l1)] * 14
         + [field(l2)] * 10
+        + [pltpu.VMEM(shape, jnp.int32)]
         + [pltpu.VMEM((12, 16, 128), jnp.float32)] * 4
+        + [pltpu.SemaphoreType.DMA((5,))]
         + [pltpu.SemaphoreType.DMA((COPIES,))] * 2,
         compiler_params=pltpu.CompilerParams(
             collective_id=0, has_side_effects=True, vmem_limit_bytes=56 * 1024 * 1024

time: 70.5 us -> 59.7 us (0.85)
  Pallas kernels: 67.1 us -> 57.4 us
  local copies, waits for them, and re-layouts: 2.57 us -> 1.49 us
    pallas_call x1, Pallas kernels: 67.1 us -> 57.4 us  [per_device(): pl.pallas_call(functools.partial(kernel, sizes), out_shape=(result, resul...]
    unnamed x4 -> x2, local copies, waits for them, and re-layouts: 2.57 us -> 1.49 us
where the time goes in v2:
time: 59.7 us; the launch traced here: 59.5 us
  Pallas kernels  57.4 us (96%)
  local copies, waits for them, and re-layouts  1.49 us (2%)
  between operations  0.64 us (1%)
    pallas_call x1, Pallas kernels, per_device(): pl.pallas_call(functools.partial(kernel, sizes), out_shape=(result, resul...  57.4 us
    unnamed x2, local copies, waits for them, and re-layouts  1.49 us

profile of v2, /device:TPU:1, one launch (start us, length us, event | category | flops | bytes accessed | tf_op | source)
XLA Modules:
  0.0 59.5 jit_solution(8299147109383202750)
XLA Ops:
  0.6 57.4 %cycle.1 = (f32[12,12,512]{2,1,0:T(8,128)S(1)}, f32[12,12,512]{2,1,0:T(8,128)S(1)}) custom-call(f32[12,12,512]{2,1,0:T(8,128)} %rhs.1, s32[12,12,512]{2,1,0:T(8,128)} %phase.1), custom_call_target="tpu_custom_call" | custom-call | flops 60000000 | bytes 1200000 | tf_op jit(solution)/shard_map/cycle/pallas_call | solution.py:502
  58.0 0.7 %copy.6 = f32[12,12,512]{2,1,0:T(8,128)} copy(f32[12,12,512]{2,1,0:T(8,128)S(1)} %get-tuple-element.2) | data formatting | bytes 589824
  58.8 0.7 %copy.7 = f32[12,12,512]{2,1,0:T(8,128)} copy(f32[12,12,512]{2,1,0:T(8,128)S(1)} %get-tuple-element.3) | data formatting | bytes 589824

commit v3 on v2

--- a/solution.py
+++ b/solution.py
@@ -98,11 +98,25 @@
     return max(offset * n, -w), min(offset * n + n, n + w)
 
 
+class Group:
+    def __init__(self, send_sem, recv_sem, blank):
+        self.send, self.recv, self.blank, self.count = send_sem, recv_sem, blank, 0
+
+    def wait(self, sem):
+        rows = self.blank.at[0 : self.count, :]
+        pltpu.make_async_copy(rows, rows, sem).wait()
+
+    def wait_recv(self):
+        self.wait(self.recv)
+
+    def wait_send(self):
+        self.wait(self.send)
+
+
 class Sender:
-    def __init__(self, send_sems, recv_sems, sizes):
-        self.send, self.recv, self.used = send_sems, recv_sems, 0
-        self.sizes = sizes
-        self.pending = []
+    def __init__(self, send_sems, recv_sems, blank, sizes):
+        self.send, self.recv, self.blank, self.sizes = send_sems, recv_sems, blank, sizes
+        self.groups = []
 
     def target(self, offset):
         place = []
@@ -111,45 +125,40 @@
             place.append(lax.rem(lax.axis_index(axis) + (o + 4 * size), size) if o else lax.axis_index(axis))
         return tuple(place)
 
-    def start(self, src, dst, offset):
+    def group(self):
+        k = len(self.groups)
+        self.groups.append(Group(self.send.at[k], self.recv.at[k], self.blank))
+        return self.groups[-1]
+
+    def start(self, group, src, dst, offset):
         copy = pltpu.make_async_remote_copy(
             src_ref=src,
             dst_ref=dst,
-            send_sem=self.send.at[self.used],
-            recv_sem=self.recv.at[self.used],
+            send_sem=group.send,
+            recv_sem=group.recv,
             device_id=self.target(offset),
             device_id_type=MESH,
         )
         copy.start()
-        self.used += 1
-        return copy
-
-    def exchange(self, ref, level, w, offsets, tiles=None, whole_y=False):
+        rows = 1
+        for size in src.shape[:-1]:
+            rows *= size
+        group.count += rows
+
+    def exchange(self, group, ref, level, w, offsets, tiles=None, whole_y=False):
         n, h = level["n"], level["h"]
         t0, t1 = tiles or (0, level["t"])
-        copies = []
         for ox, oy in offsets:
             x0, x1 = reach(ox, n, w - near(oy, n))
             y0, y1 = (-w, n + w) if whole_y else reach(oy, n, w - near(ox, n))
             sx, sy = x0 - ox * n + h, y0 - oy * n + h
-            copies.append(
-                self.start(
-                    ref.at[sx : sx + x1 - x0, t0:t1, sy : sy + y1 - y0, :],
-                    ref.at[x0 + h : x1 + h, t0:t1, y0 + h : y1 + h, :],
-                    (-ox, -oy, 0),
-                )
+            self.start(
+                group,
+                ref.at[sx : sx + x1 - x0, t0:t1, sy : sy + y1 - y0, :],
+                ref.at[x0 + h : x1 + h, t0:t1, y0 + h : y1 + h, :],
+                (-ox, -oy, 0),
             )
-        return copies
-
-
-def wait_recv(copies):
-    for copy in copies:
-        copy.wait_recv()
-
-
-def wait_send(copies):
-    for copy in copies:
-        copy.wait_send()
+        return group
 
 
 def diamond(n, w, most):
@@ -186,8 +195,13 @@
         pl.when(gy == sizes["gy"] - 1 - k)(functools.partial(clear, *every, *above))
 
 
+def inverse_of(value):
+    guess = pl.reciprocal(value, approx=True)
+    return guess * (2.0 - value * guess)
+
+
 def conduct(a, b, scale):
-    return scale / jnp.maximum(a + b, 0.5)
+    return scale * inverse_of(jnp.maximum(a + b, 0.5))
 
 
 def coefficients(rho, co, level, w, scale, unroll):
@@ -208,7 +222,7 @@
         bzp[i, :, ys, :] = above
         bzm[i, :, ys, :] = below
         total = (before + after) + (above + below) + (by[i, :, ys, :] + by[i, :, pl.ds(lo - 1, rows), :])
-        inverse = jnp.where(here > 0.0, 1.0 / total, 0.0)
+        inverse = jnp.where(here > 0.0, inverse_of(total), 0.0)
         iv[i, :, ys, :] = inverse
         return after
 
@@ -314,9 +328,9 @@
     co1 = take(5)
     rho2, r2, x2, d21, d22 = take(5)
     co2 = take(5)
-    kind, zs_up, zs_down, zr_below, zr_above, local_sems, send_sems, recv_sems = take(8)
+    kind, zs_up, zs_down, zr_below, zr_above, blank, local_sems, send_sems, recv_sems = take(9)
     l0, l1, l2 = LEVELS
-    sender = Sender(send_sems, recv_sems, sizes)
+    sender = Sender(send_sems, recv_sems, blank, sizes)
     first, pairs = weights(SMOOTH_LOWEST, DEGREE)
     first2, pairs2 = weights(COARSE_LOWEST, COARSE_ITERS)
     own = slice(l0["h"], l0["h"] + 12)
@@ -355,13 +369,12 @@
     columns(0, 12, 4, prepare, 0)
     pl.semaphore_wait(barrier, len(met))
 
-    along_z = [
-        sender.start(zs_up.at[:, :12, :], zr_below.at[:, :12, :], (0, 0, 1)),
-        sender.start(zs_down.at[:, :12, :], zr_above.at[:, :12, :], (0, 0, -1)),
-    ]
-    fine_rho = sender.exchange(rho0, l0, 5, AROUND, (0, 4))
-
-    wait_recv(along_z)
+    along_z = sender.group()
+    sender.start(along_z, zs_up.at[:, :12, :], zr_below.at[:, :12, :], (0, 0, 1))
+    sender.start(along_z, zs_down.at[:, :12, :], zr_above.at[:, :12, :], (0, 0, -1))
+    fine_rho = sender.exchange(sender.group(), rho0, l0, 5, AROUND, (0, 4))
+
+    along_z.wait_recv()
     gz = lax.axis_index("gz")
     inside = jnp.where(lane < 64, jnp.where(gz == sizes["gz"] - 1, 0.0, 1.0), jnp.where(gz == 0, 0.0, 1.0))
 
@@ -372,45 +385,45 @@
         return c
 
     columns(0, 12, 6, ends, 0)
-    fine_rho += sender.exchange(rho0, l0, 5, AROUND, (4, 5))
-    fine_r = sender.exchange(r0, l0, 4, AROUND)
+    fine_rho4 = sender.exchange(sender.group(), rho0, l0, 5, AROUND, (4, 5))
+    fine_r = sender.exchange(sender.group(), r0, l0, 4, AROUND)
 
     restricted(rho0, rho1, l0, l1)
     restricted(rho1, rho2, l1, l2)
-    density1 = sender.exchange(rho1, l1, 7, diamond(6, 7, 2))
-    density2 = sender.exchange(rho2, l2, 8, line_y2)
-
-    wait_recv(fine_rho)
-    wait_send(fine_rho)
+    density1 = sender.exchange(sender.group(), rho1, l1, 7, diamond(6, 7, 2))
+    density2 = sender.exchange(sender.group(), rho2, l2, 8, line_y2)
+
+    fine_rho.wait_recv()
+    fine_rho4.wait_recv()
     clear_outside(rho0, l0, 5, sizes)
-    coefficients(rho0, co0, l0, 4, 2.0, 1)
-    wait_recv(fine_r)
-    wait_send(fine_r)
+    coefficients(rho0, co0, l0, 4, 2.0, 2)
+    fine_r.wait_recv()
+    fine_r.wait_send()
     begin(r0, co0[4], d01, l0, 4, first, 4)
-    smooth(d01, r0, d02, co0, l0, 3, *pairs[0], 3)
-    smooth(d02, r0, d03, co0, l0, 2, *pairs[1], 4)
-    smooth(d03, r0, d04, co0, l0, 1, *pairs[2], 4)
+    smooth(d01, r0, d02, co0, l0, 3, *pairs[0], 9)
+    smooth(d02, r0, d03, co0, l0, 2, *pairs[1], 8)
+    smooth(d03, r0, d04, co0, l0, 1, *pairs[2], 7)
 
     def finish_down0(i, ys, here, applied):
         up0[i, :, ys, :] = r0[i, :, ys, :] - applied
         x0[i, :, ys, :] = (d01[i, :, ys, :] + d02[i, :, ys, :]) + (d03[i, :, ys, :] + here)
 
-    sweep(d04, co0, l0, 0, 4, finish_down0)
+    sweep(d04, co0, l0, 0, 6, finish_down0)
 
     restricted(up0, r1, l0, l1)
-    second = sender.exchange(r1, l1, 4, AROUND)
-    wait_recv(density2)
-    density2x = sender.exchange(rho2, l2, 8, line_x2, whole_y=True)
-    back0 = sender.exchange(up0, l0, 4, AROUND)
-    wait_recv(density1)
-    wait_send(density1)
+    second = sender.exchange(sender.group(), r1, l1, 4, AROUND)
+    density2.wait_recv()
+    density2x = sender.exchange(sender.group(), rho2, l2, 8, line_x2, whole_y=True)
+    back0 = sender.exchange(sender.group(), up0, l0, 4, AROUND)
+    density1.wait_recv()
+    density1.wait_send()
     clear_outside(rho1, l1, 7, sizes)
     coefficients(rho1, co1, l1, 6, 0.5, 2)
-    wait_recv(second)
-    wait_send(second)
+    second.wait_recv()
+    second.wait_send()
     begin(r1, co1[4], d11, l1, 4, first, 7)
-    smooth(d11, r1, d12, co1, l1, 3, *pairs[0], 6)
-    smooth(d12, r1, d13, co1, l1, 2, *pairs[1], 5)
+    smooth(d11, r1, d12, co1, l1, 3, *pairs[0], 12)
+    smooth(d12, r1, d13, co1, l1, 2, *pairs[1], 10)
     smooth(d13, r1, d14, co1, l1, 1, *pairs[2], 8)
 
     def finish_down1(i, ys, here, applied):
@@ -420,14 +433,16 @@
     sweep(d14, co1, l1, 0, 6, finish_down1)
 
     restricted(up1, r2, l1, l2)
-    third = sender.exchange(r2, l2, 7, coarse_offsets)
-    back1 = sender.exchange(up1, l1, 6, AROUND) + sender.exchange(x1, l1, 3, AROUND)
-    wait_recv(density2x)
-    wait_send(density2 + density2x)
+    third = sender.exchange(sender.group(), r2, l2, 7, coarse_offsets)
+    back1 = sender.exchange(sender.group(), up1, l1, 6, AROUND)
+    sender.exchange(back1, x1, l1, 3, AROUND)
+    density2x.wait_recv()
+    density2.wait_send()
+    density2x.wait_send()
     clear_outside(rho2, l2, 8, sizes)
     coefficients(rho2, co2, l2, 7, 0.125, 2)
-    wait_recv(third)
-    wait_send(third)
+    third.wait_recv()
+    third.wait_send()
     begin(r2, co2[4], d21, l2, 7, first2, 17)
 
     def copy_total(i, c):
@@ -437,7 +452,7 @@
     columns(l2["h"], l2["h"] + 3, 3, copy_total, 0)
     v, d = d21, d22
     for k, (alpha, beta) in enumerate(pairs2):
-        smooth(v, r2, d, co2, l2, 6 - k, alpha, beta, 8)
+        smooth(v, r2, d, co2, l2, 6 - k, alpha, beta, 15)
         v, d = d, v
 
         def add_total(i, c, v=v):
@@ -446,16 +461,16 @@
 
         columns(l2["h"], l2["h"] + 3, 3, add_total, 0)
 
-    fourth = sender.exchange(x2, l2, 4, diamond(3, 4, 2))
-    wait_recv(back1)
-    wait_send(back1)
-    wait_recv(fourth)
+    fourth = sender.exchange(sender.group(), x2, l2, 4, diamond(3, 4, 2))
+    back1.wait_recv()
+    back1.wait_send()
+    fourth.wait_recv()
     clear_outside(x2, l2, 4, sizes)
     prolonged(x2, u1, l2, l1, 4)
-    smooth(u1, up1, d11, co1, l1, 6, None, first, 6)
+    smooth(u1, up1, d11, co1, l1, 6, None, first, 9)
     smooth(d11, up1, d12, co1, l1, 5, *pairs[0], 8)
-    smooth(d12, up1, d13, co1, l1, 4, *pairs[1], 7)
-    smooth(d13, up1, d14, co1, l1, 3, *pairs[2], 6)
+    smooth(d12, up1, d13, co1, l1, 4, *pairs[1], 14)
+    smooth(d13, up1, d14, co1, l1, 3, *pairs[2], 12)
     reach1 = pl.ds(l1["h"] - 3, 12)
 
     def finish_up1(i, c):
@@ -467,12 +482,12 @@
     clear_outside(x1, l1, 3, sizes)
 
     prolonged(x1, u0, l1, l0, 3)
-    wait_recv(back0)
-    wait_send(back0)
-    smooth(u0, up0, d01, co0, l0, 4, None, first, 3)
-    smooth(d01, up0, d02, co0, l0, 3, *pairs[0], 3)
-    smooth(d02, up0, d03, co0, l0, 2, *pairs[1], 4)
-    smooth(d03, up0, d04, co0, l0, 1, *pairs[2], 4)
+    back0.wait_recv()
+    back0.wait_send()
+    smooth(u0, up0, d01, co0, l0, 4, None, first, 10)
+    smooth(d01, up0, d02, co0, l0, 3, *pairs[0], 9)
+    smooth(d02, up0, d03, co0, l0, 2, *pairs[1], 8)
+    smooth(d03, up0, d04, co0, l0, 1, *pairs[2], 7)
 
     def finish_up0(i, ys, here, applied):
         j = i - l0["h"]
@@ -483,12 +498,14 @@
             out_x[j, :, 128 * t : 128 * t + 128] = total[t]
             out_r[j, :, 128 * t : 128 * t + 128] = rest[t]
 
-    sweep(d04, co0, l0, 0, 4, finish_up0)
-    wait_send(along_z)
-    wait_send(fourth)
-
-
-COPIES = 2 + 24 + 12 + 12 + 8 + 6 + 8 + 24 + 16 + 12
+    sweep(d04, co0, l0, 0, 6, finish_up0)
+    along_z.wait_send()
+    fine_rho.wait_send()
+    fine_rho4.wait_send()
+    fourth.wait_send()
+
+
+GROUPS = 12
 
 
 def per_device(sizes, right_side, phase):
@@ -509,8 +526,9 @@
         + [field(l2)] * 10
         + [pltpu.VMEM(shape, jnp.int32)]
         + [pltpu.VMEM((12, 16, 128), jnp.float32)] * 4
+        + [pltpu.VMEM((1280, 128), jnp.float32)]
         + [pltpu.SemaphoreType.DMA((5,))]
-        + [pltpu.SemaphoreType.DMA((COPIES,))] * 2,
+        + [pltpu.SemaphoreType.DMA((GROUPS,))] * 2,
         compiler_params=pltpu.CompilerParams(
             collective_id=0, has_side_effects=True, vmem_limit_bytes=56 * 1024 * 1024
         ),

time: 59.7 us -> 55.6 us (0.931)
  Pallas kernels: 57.4 us -> 53.4 us
    pallas_call x1, Pallas kernels: 57.4 us -> 53.4 us  [per_device(): pl.pallas_call(functools.partial(kernel, sizes), out_shape=(result, resul...]
where the time goes in v3:
time: 55.6 us; the launch traced here: 55.5 us
  Pallas kernels  53.4 us (96%)
  local copies, waits for them, and re-layouts  1.49 us (3%)
  between operations  0.64 us (1%)
    pallas_call x1, Pallas kernels, per_device(): pl.pallas_call(functools.partial(kernel, sizes), out_shape=(result, resul...  53.4 us
    unnamed x2, local copies, waits for them, and re-layouts  1.49 us

profile of v3, /device:TPU:1, one launch (start us, length us, event | category | flops | bytes accessed | tf_op | source)
XLA Modules:
  0.0 55.5 jit_solution(14638665449292636128)
XLA Ops:
  0.6 53.4 %cycle.1 = (f32[12,12,512]{2,1,0:T(8,128)S(1)}, f32[12,12,512]{2,1,0:T(8,128)S(1)}) custom-call(f32[12,12,512]{2,1,0:T(8,128)} %rhs.1, s32[12,12,512]{2,1,0:T(8,128)} %phase.1), custom_call_target="tpu_custom_call" | custom-call | flops 60000000 | bytes 1200000 | tf_op jit(solution)/shard_map/cycle/pallas_call | solution.py:519
  54.0 0.7 %copy.6 = f32[12,12,512]{2,1,0:T(8,128)} copy(f32[12,12,512]{2,1,0:T(8,128)S(1)} %get-tuple-element.2) | data formatting | bytes 589824
  54.7 0.7 %copy.7 = f32[12,12,512]{2,1,0:T(8,128)} copy(f32[12,12,512]{2,1,0:T(8,128)S(1)} %get-tuple-element.3) | data formatting | bytes 589824

commit v4 on v3

--- a/solution.py
+++ b/solution.py
@@ -171,16 +171,19 @@
 
 
 AROUND = diamond(1, 2, 1)
-
-
-def clear_outside(ref, level, w, sizes):
-    n, h, t = level["n"], level["h"], level["t"]
+FACES = [o for o in AROUND if 0 in o]
+CORNERS = [o for o in AROUND if 0 not in o]
+
+
+def clear_outside(ref, level, w, sizes, tiles=None):
+    n, h = level["n"], level["h"]
+    t0, t1 = tiles or (0, level["t"])
 
     def clear(x0, x1, y0, y1):
-        zero = jnp.zeros((t, y1 - y0, 128), jnp.float32)
+        zero = jnp.zeros((t1 - t0, y1 - y0, 128), jnp.float32)
 
         def body(i, c):
-            ref[i, :, y0:y1, :] = zero
+            ref[i, t0:t1, y0:y1, :] = zero
             return c
 
         lax.fori_loop(x0, x1, body, 0)
@@ -204,31 +207,43 @@
     return scale * inverse_of(jnp.maximum(a + b, 0.5))
 
 
-def coefficients(rho, co, level, w, scale, unroll):
+def face_coefficients(rho, co, level, w, scale, unroll, tiles=None):
+    bx, by = co[:2]
+    n, h = level["n"], level["h"]
+    lo, hi, rows = h - w, h + n + w, n + 2 * w
+    ts, ys, ends = slice(*(tiles or (0, level["t"]))), pl.ds(lo, rows), pl.ds(lo - 1, rows + 1)
+
+    def body(i, c):
+        bx[i, ts, ys, :] = conduct(rho[i, ts, ys, :], rho[i + 1, ts, ys, :], scale)
+        by[i, ts, ends, :] = conduct(rho[i, ts, ends, :], rho[i, ts, pl.ds(lo, rows + 1), :], scale)
+        return c
+
+    bx[lo - 1, ts, ys, :] = conduct(rho[lo - 1, ts, ys, :], rho[lo, ts, ys, :], scale)
+    columns(lo, hi, unroll, body, 0)
+
+
+def other_coefficients(rho, co, level, w, scale, unroll):
     bx, by, bzp, bzm, iv = co
     n, h = level["n"], level["h"]
     lo, hi, rows = h - w, h + n + w, n + 2 * w
     ys = pl.ds(lo, rows)
 
-    def body(i, before):
+    def body(i, c):
         here = rho[i, :, ys, :]
-        after = conduct(here, rho[i + 1, :, ys, :], scale)
-        bx[i, :, ys, :] = after
-        by[i, :, pl.ds(lo - 1, rows + 1), :] = conduct(
-            rho[i, :, pl.ds(lo - 1, rows + 1), :], rho[i, :, pl.ds(lo, rows + 1), :], scale
-        )
         above = jnp.stack([conduct(a, b, scale) for a, b in zip(split(here), shifted(split(here), 1))])
         below = jnp.stack(shifted(split(above), -1))
         bzp[i, :, ys, :] = above
         bzm[i, :, ys, :] = below
-        total = (before + after) + (above + below) + (by[i, :, ys, :] + by[i, :, pl.ds(lo - 1, rows), :])
-        inverse = jnp.where(here > 0.0, inverse_of(total), 0.0)
-        iv[i, :, ys, :] = inverse
-        return after
-
-    start = conduct(rho[lo - 1, :, ys, :], rho[lo, :, ys, :], scale)
-    bx[lo - 1, :, ys, :] = start
-    columns(lo, hi, unroll, body, start)
+        total = (bx[i - 1, :, ys, :] + bx[i, :, ys, :]) + (by[i, :, ys, :] + by[i, :, pl.ds(lo - 1, rows), :])
+        iv[i, :, ys, :] = jnp.where(here > 0.0, inverse_of(total + (above + below)), 0.0)
+        return c
+
+    columns(lo, hi, unroll, body, 0)
+
+
+def coefficients(rho, co, level, w, scale, unroll):
+    face_coefficients(rho, co, level, w, scale, unroll)
+    other_coefficients(rho, co, level, w, scale, unroll)
 
 
 def begin(r, iv, d, level, w, weight, unroll):
@@ -312,7 +327,7 @@
                     fine[h - 2 * w + 2 * k + x, t, pl.ds(h - 2 * w + y, count, stride=2), :] = v
         return c
 
-    columns(0, count, 3, body, 0)
+    columns(0, count, 6, body, 0)
 
 
 def kernel(sizes, rhs, phase, out_x, out_r, *scratch):
@@ -346,10 +361,18 @@
     coarse_offsets = diamond(3, 7, 3)
     line_y2 = [(0, o) for o in (3, -3, 2, -2, 1, -1)]
     line_x2 = [(o, 0) for _, o in line_y2]
-    met = {(ox, oy, 0) for ox, oy in coarse_offsets + line_y2 + line_x2 + AROUND} | {(0, 0, 1), (0, 0, -1)}
+    met = sorted({(ox, oy, 0) for ox, oy in coarse_offsets + line_y2 + line_x2 + AROUND})
+    gz = lax.axis_index("gz")
+    has_below, has_above = gz > 0, gz < sizes["gz"] - 1
     barrier = pltpu.get_barrier_semaphore()
-    for offset in sorted(met):
+
+    def greet(offset):
         pl.semaphore_signal(barrier, inc=1, device_id=sender.target(offset), device_id_type=MESH)
+
+    pl.when(has_above)(lambda: greet((0, 0, 1)))
+    pl.when(has_below)(lambda: greet((0, 0, -1)))
+    for offset in met:
+        greet(offset)
 
     lane = lanes((12, 128))
     for copy in loads:
@@ -367,16 +390,33 @@
         return c
 
     columns(0, 12, 4, prepare, 0)
-    pl.semaphore_wait(barrier, len(met))
-
-    along_z = sender.group()
-    sender.start(along_z, zs_up.at[:, :12, :], zr_below.at[:, :12, :], (0, 0, 1))
-    sender.start(along_z, zs_down.at[:, :12, :], zr_above.at[:, :12, :], (0, 0, -1))
+    beside = jnp.where(has_below, 1, 0) + jnp.where(has_above, 1, 0)
+    pl.semaphore_wait(barrier, len(met) + beside)
+
+    upwards, downwards = sender.group(), sender.group()
+
+    @pl.when(has_above)
+    def _():
+        sender.start(upwards, zs_up.at[:, :12, :], zr_below.at[:, :12, :], (0, 0, 1))
+
+    @pl.when(has_below)
+    def _():
+        sender.start(downwards, zs_down.at[:, :12, :], zr_above.at[:, :12, :], (0, 0, -1))
+
+    @pl.when(jnp.logical_not(has_below))
+    def _():
+        zr_below[...] = jnp.zeros_like(zr_below)
+
+    @pl.when(jnp.logical_not(has_above))
+    def _():
+        zr_above[...] = jnp.zeros_like(zr_above)
+
     fine_rho = sender.exchange(sender.group(), rho0, l0, 5, AROUND, (0, 4))
-
-    along_z.wait_recv()
-    gz = lax.axis_index("gz")
-    inside = jnp.where(lane < 64, jnp.where(gz == sizes["gz"] - 1, 0.0, 1.0), jnp.where(gz == 0, 0.0, 1.0))
+    fine_r = sender.exchange(sender.group(), r0, l0, 4, FACES, (0, 4))
+
+    pl.when(has_below)(upwards.wait_recv)
+    pl.when(has_above)(downwards.wait_recv)
+    inside = jnp.where(lane < 64, jnp.where(has_above, 1.0, 0.0), jnp.where(has_below, 1.0, 0.0))
 
     def ends(i, c):
         below, above = zr_below[i, :12, :], zr_above[i, :12, :]
@@ -386,7 +426,8 @@
 
     columns(0, 12, 6, ends, 0)
     fine_rho4 = sender.exchange(sender.group(), rho0, l0, 5, AROUND, (4, 5))
-    fine_r = sender.exchange(sender.group(), r0, l0, 4, AROUND)
+    sender.exchange(fine_r, r0, l0, 4, CORNERS)
+    sender.exchange(fine_r, r0, l0, 4, FACES, (4, 5))
 
     restricted(rho0, rho1, l0, l1)
     restricted(rho1, rho2, l1, l2)
@@ -394,9 +435,12 @@
     density2 = sender.exchange(sender.group(), rho2, l2, 8, line_y2)
 
     fine_rho.wait_recv()
+    clear_outside(rho0, l0, 5, sizes, (0, 4))
+    face_coefficients(rho0, co0, l0, 4, 2.0, 2, (0, 4))
     fine_rho4.wait_recv()
-    clear_outside(rho0, l0, 5, sizes)
-    coefficients(rho0, co0, l0, 4, 2.0, 2)
+    clear_outside(rho0, l0, 5, sizes, (4, 5))
+    face_coefficients(rho0, co0, l0, 4, 2.0, 5, (4, 5))
+    other_coefficients(rho0, co0, l0, 4, 2.0, 2)
     fine_r.wait_recv()
     fine_r.wait_send()
     begin(r0, co0[4], d01, l0, 4, first, 4)
@@ -499,13 +543,14 @@
             out_r[j, :, 128 * t : 128 * t + 128] = rest[t]
 
     sweep(d04, co0, l0, 0, 6, finish_up0)
-    along_z.wait_send()
+    pl.when(has_above)(upwards.wait_send)
+    pl.when(has_below)(downwards.wait_send)
     fine_rho.wait_send()
     fine_rho4.wait_send()
     fourth.wait_send()
 
 
-GROUPS = 12
+GROUPS = 13
 
 
 def per_device(sizes, right_side, phase):

time: 55.6 us -> 49.3 us (0.89)
  Pallas kernels: 53.4 us -> 47.1 us
    pallas_call x1, Pallas kernels: 53.4 us -> 47.1 us  [per_device(): pl.pallas_call(functools.partial(kernel, sizes), out_shape=(result, resul...]
where the time goes in v4:
time: 49.3 us; the launch traced here: 49.2 us
  Pallas kernels  47.1 us (96%)
  local copies, waits for them, and re-layouts  1.49 us (3%)
  between operations  0.64 us (1%)
    pallas_call x1, Pallas kernels, per_device(): pl.pallas_call(functools.partial(kernel, sizes), out_shape=(result, resul...  47.1 us
    unnamed x2, local copies, waits for them, and re-layouts  1.49 us

profile of v4, /device:TPU:1, one launch (start us, length us, event | category | flops | bytes accessed | tf_op | source)
XLA Modules:
  0.0 49.2 jit_solution(9320298658935368684)
XLA Ops:
  0.6 47.1 %cycle.1 = (f32[12,12,512]{2,1,0:T(8,128)S(1)}, f32[12,12,512]{2,1,0:T(8,128)S(1)}) custom-call(f32[12,12,512]{2,1,0:T(8,128)} %rhs.1, s32[12,12,512]{2,1,0:T(8,128)} %phase.1), custom_call_target="tpu_custom_call" | custom-call | flops 60000000 | bytes 1200000 | tf_op jit(solution)/shard_map/cycle/pallas_call | solution.py:564
  47.7 0.7 %copy.6 = f32[12,12,512]{2,1,0:T(8,128)} copy(f32[12,12,512]{2,1,0:T(8,128)S(1)} %get-tuple-element.2) | data formatting | bytes 589824
  48.5 0.7 %copy.7 = f32[12,12,512]{2,1,0:T(8,128)} copy(f32[12,12,512]{2,1,0:T(8,128)S(1)} %get-tuple-element.3) | data formatting | bytes 589824

commit v5 on v4

--- a/solution.py
+++ b/solution.py
@@ -140,25 +140,42 @@
             device_id_type=MESH,
         )
         copy.start()
-        rows = 1
-        for size in src.shape[:-1]:
-            rows *= size
-        group.count += rows
-
-    def exchange(self, group, ref, level, w, offsets, tiles=None, whole_y=False):
+
+    def exchange(self, group, ref, level, w, offsets, tiles=None, whole_y=False, zeros=None, cut=False):
         n, h = level["n"], level["h"]
         t0, t1 = tiles or (0, level["t"])
         for ox, oy in offsets:
-            x0, x1 = reach(ox, n, w - near(oy, n))
-            y0, y1 = (-w, n + w) if whole_y else reach(oy, n, w - near(ox, n))
-            sx, sy = x0 - ox * n + h, y0 - oy * n + h
-            self.start(
-                group,
-                ref.at[sx : sx + x1 - x0, t0:t1, sy : sy + y1 - y0, :],
-                ref.at[x0 + h : x1 + h, t0:t1, y0 + h : y1 + h, :],
-                (-ox, -oy, 0),
-            )
+            spans = [(reach(ox, n, w - near(oy, n)), (-w, n + w) if whole_y else reach(oy, n, w - near(ox, n)))]
+            if cut and ox and oy:
+                low, high = reach(ox, n, 2), reach(ox, n, w - 1)
+                rest = (high[0], low[0]) if ox < 0 else (low[1], high[1])
+                spans = [(low, reach(oy, n, w - 1)), (rest, reach(oy, n, w - 3))]
+            for (x0, x1), (y0, y1) in spans:
+                self.block(group, ref, (x1 - x0, t0, t1, y1 - y0), (x0, y0), (ox * n, oy * n), h, (-ox, -oy, 0), zeros)
         return group
+
+    def block(self, group, ref, shape, corner, shift, h, offset, zeros):
+        x, t0, t1, y = shape
+        dx, dy = corner[0] + h, corner[1] + h
+        sx, sy = dx - shift[0], dy - shift[1]
+        dst = ref.at[dx : dx + x, t0:t1, dy : dy + y, :]
+
+        def send(src):
+            self.start(group, src, dst, offset)
+
+        group.count += x * (t1 - t0) * y
+        src = ref.at[sx : sx + x, t0:t1, sy : sy + y, :]
+        if zeros is None:
+            send(src)
+            return
+        outside = None
+        for axis, o in zip(("gx", "gy"), offset):
+            if o:
+                place = lax.axis_index(axis) + o
+                beyond = place < 0 if o < 0 else place >= self.sizes[axis]
+                outside = beyond if outside is None else jnp.logical_or(outside, beyond)
+        pl.when(outside)(lambda: send(zeros.at[0:x, 0 : t1 - t0, 0:y, :]))
+        pl.when(jnp.logical_not(outside))(lambda: send(src))
 
 
 def diamond(n, w, most):
@@ -173,29 +190,6 @@
 AROUND = diamond(1, 2, 1)
 FACES = [o for o in AROUND if 0 in o]
 CORNERS = [o for o in AROUND if 0 not in o]
-
-
-def clear_outside(ref, level, w, sizes, tiles=None):
-    n, h = level["n"], level["h"]
-    t0, t1 = tiles or (0, level["t"])
-
-    def clear(x0, x1, y0, y1):
-        zero = jnp.zeros((t1 - t0, y1 - y0, 128), jnp.float32)
-
-        def body(i, c):
-            ref[i, t0:t1, y0:y1, :] = zero
-            return c
-
-        lax.fori_loop(x0, x1, body, 0)
-
-    gx, gy = lax.axis_index("gx"), lax.axis_index("gy")
-    for k in range(-(-w // n)):
-        below, above = (h - w, h - k * n), (h + n + k * n, h + n + w)
-        every = (h - w, h + n + w)
-        pl.when(gx == k)(functools.partial(clear, *below, *every))
-        pl.when(gx == sizes["gx"] - 1 - k)(functools.partial(clear, *above, *every))
-        pl.when(gy == k)(functools.partial(clear, *every, *below))
-        pl.when(gy == sizes["gy"] - 1 - k)(functools.partial(clear, *every, *above))
 
 
 def inverse_of(value):
@@ -330,7 +324,7 @@
     columns(0, count, 6, body, 0)
 
 
-def kernel(sizes, rhs, phase, out_x, out_r, *scratch):
+def kernel(sizes, rhs, phase, out, *scratch):
     scratch = list(scratch)
 
     def take(count):
@@ -343,7 +337,7 @@
     co1 = take(5)
     rho2, r2, x2, d21, d22 = take(5)
     co2 = take(5)
-    kind, zs_up, zs_down, zr_below, zr_above, blank, local_sems, send_sems, recv_sems = take(9)
+    kind, zs_up, zs_down, zr_below, zr_above, blank, zeros, local_sems, send_sems, recv_sems = take(10)
     l0, l1, l2 = LEVELS
     sender = Sender(send_sems, recv_sems, blank, sizes)
     first, pairs = weights(SMOOTH_LOWEST, DEGREE)
@@ -373,6 +367,8 @@
     pl.when(has_below)(lambda: greet((0, 0, -1)))
     for offset in met:
         greet(offset)
+
+    zeros[...] = jnp.zeros_like(zeros)
 
     lane = lanes((12, 128))
     for copy in loads:
@@ -394,6 +390,7 @@
     pl.semaphore_wait(barrier, len(met) + beside)
 
     upwards, downwards = sender.group(), sender.group()
+    upwards.count = downwards.count = 12 * 12
 
     @pl.when(has_above)
     def _():
@@ -411,7 +408,7 @@
     def _():
         zr_above[...] = jnp.zeros_like(zr_above)
 
-    fine_rho = sender.exchange(sender.group(), rho0, l0, 5, AROUND, (0, 4))
+    fine_rho = sender.exchange(sender.group(), rho0, l0, 5, AROUND, (0, 4), zeros=zeros, cut=True)
     fine_r = sender.exchange(sender.group(), r0, l0, 4, FACES, (0, 4))
 
     pl.when(has_below)(upwards.wait_recv)
@@ -425,20 +422,18 @@
         return c
 
     columns(0, 12, 6, ends, 0)
-    fine_rho4 = sender.exchange(sender.group(), rho0, l0, 5, AROUND, (4, 5))
-    sender.exchange(fine_r, r0, l0, 4, CORNERS)
+    fine_rho4 = sender.exchange(sender.group(), rho0, l0, 5, AROUND, (4, 5), zeros=zeros, cut=True)
+    sender.exchange(fine_r, r0, l0, 4, CORNERS, cut=True)
     sender.exchange(fine_r, r0, l0, 4, FACES, (4, 5))
 
     restricted(rho0, rho1, l0, l1)
     restricted(rho1, rho2, l1, l2)
-    density1 = sender.exchange(sender.group(), rho1, l1, 7, diamond(6, 7, 2))
-    density2 = sender.exchange(sender.group(), rho2, l2, 8, line_y2)
+    density1 = sender.exchange(sender.group(), rho1, l1, 7, diamond(6, 7, 2), zeros=zeros)
+    density2 = sender.exchange(sender.group(), rho2, l2, 8, line_y2, zeros=zeros)
 
     fine_rho.wait_recv()
-    clear_outside(rho0, l0, 5, sizes, (0, 4))
     face_coefficients(rho0, co0, l0, 4, 2.0, 2, (0, 4))
     fine_rho4.wait_recv()
-    clear_outside(rho0, l0, 5, sizes, (4, 5))
     face_coefficients(rho0, co0, l0, 4, 2.0, 5, (4, 5))
     other_coefficients(rho0, co0, l0, 4, 2.0, 2)
     fine_r.wait_recv()
@@ -457,12 +452,11 @@
     restricted(up0, r1, l0, l1)
     second = sender.exchange(sender.group(), r1, l1, 4, AROUND)
     density2.wait_recv()
-    density2x = sender.exchange(sender.group(), rho2, l2, 8, line_x2, whole_y=True)
-    back0 = sender.exchange(sender.group(), up0, l0, 4, AROUND)
+    density2x = sender.exchange(sender.group(), rho2, l2, 8, line_x2, whole_y=True, zeros=zeros)
     density1.wait_recv()
     density1.wait_send()
-    clear_outside(rho1, l1, 7, sizes)
     coefficients(rho1, co1, l1, 6, 0.5, 2)
+    back0 = sender.exchange(sender.group(), up0, l0, 4, AROUND)
     second.wait_recv()
     second.wait_send()
     begin(r1, co1[4], d11, l1, 4, first, 7)
@@ -478,13 +472,12 @@
 
     restricted(up1, r2, l1, l2)
     third = sender.exchange(sender.group(), r2, l2, 7, coarse_offsets)
-    back1 = sender.exchange(sender.group(), up1, l1, 6, AROUND)
-    sender.exchange(back1, x1, l1, 3, AROUND)
     density2x.wait_recv()
     density2.wait_send()
     density2x.wait_send()
-    clear_outside(rho2, l2, 8, sizes)
     coefficients(rho2, co2, l2, 7, 0.125, 2)
+    back1 = sender.exchange(sender.group(), up1, l1, 6, AROUND)
+    sender.exchange(back1, x1, l1, 3, AROUND, zeros=zeros)
     third.wait_recv()
     third.wait_send()
     begin(r2, co2[4], d21, l2, 7, first2, 17)
@@ -505,25 +498,22 @@
 
         columns(l2["h"], l2["h"] + 3, 3, add_total, 0)
 
-    fourth = sender.exchange(sender.group(), x2, l2, 4, diamond(3, 4, 2))
+    fourth = sender.exchange(sender.group(), x2, l2, 4, diamond(3, 4, 2), zeros=zeros)
     back1.wait_recv()
     back1.wait_send()
     fourth.wait_recv()
-    clear_outside(x2, l2, 4, sizes)
     prolonged(x2, u1, l2, l1, 4)
     smooth(u1, up1, d11, co1, l1, 6, None, first, 9)
     smooth(d11, up1, d12, co1, l1, 5, *pairs[0], 8)
     smooth(d12, up1, d13, co1, l1, 4, *pairs[1], 14)
-    smooth(d13, up1, d14, co1, l1, 3, *pairs[2], 12)
-    reach1 = pl.ds(l1["h"] - 3, 12)
-
-    def finish_up1(i, c):
-        total = (x1[i, :, reach1, :] + u1[i, :, reach1, :]) + (d11[i, :, reach1, :] + d12[i, :, reach1, :])
-        x1[i, :, reach1, :] = total + (d13[i, :, reach1, :] + d14[i, :, reach1, :])
-        return c
-
-    columns(l1["h"] - 3, l1["h"] + 9, 6, finish_up1, 0)
-    clear_outside(x1, l1, 3, sizes)
+    alpha, beta = pairs[2]
+
+    def finish_up1(i, ys, here, applied):
+        new = alpha * here + beta * (co1[4][i, :, ys, :] * (up1[i, :, ys, :] - applied))
+        total = (x1[i, :, ys, :] + u1[i, :, ys, :]) + (d11[i, :, ys, :] + d12[i, :, ys, :])
+        x1[i, :, ys, :] = total + (here + new)
+
+    sweep(d13, co1, l1, 3, 12, finish_up1)
 
     prolonged(x1, u0, l1, l0, 3)
     back0.wait_recv()
@@ -539,8 +529,8 @@
         total = total + (d03[i, :, ys, :] + here)
         rest = up0[i, :, ys, :] - applied
         for t in range(4):
-            out_x[j, :, 128 * t : 128 * t + 128] = total[t]
-            out_r[j, :, 128 * t : 128 * t + 128] = rest[t]
+            out[0, j, :, 128 * t : 128 * t + 128] = total[t]
+            out[1, j, :, 128 * t : 128 * t + 128] = rest[t]
 
     sweep(d04, co0, l0, 0, 6, finish_up0)
     pl.when(has_above)(upwards.wait_send)
@@ -561,17 +551,17 @@
     shape = right_side.shape
     result = pltpu.VMEM(shape, jnp.float32)
     whole = pl.BlockSpec(memory_space=pltpu.VMEM)
-    return pl.pallas_call(
+    both = pl.pallas_call(
         functools.partial(kernel, sizes),
-        out_shape=(result, result),
+        out_shape=pltpu.VMEM((2,) + shape, jnp.float32),
         in_specs=[pl.BlockSpec(memory_space=pl.ANY)] * 2,
-        out_specs=(whole, whole),
+        out_specs=whole,
         scratch_shapes=[field(l0)] * 14
         + [field(l1)] * 14
         + [field(l2)] * 10
         + [pltpu.VMEM(shape, jnp.int32)]
         + [pltpu.VMEM((12, 16, 128), jnp.float32)] * 4
-        + [pltpu.VMEM((1280, 128), jnp.float32)]
+        + [pltpu.VMEM((1280, 128), jnp.float32), pltpu.VMEM((12, 4, 24, 128), jnp.float32)]
         + [pltpu.SemaphoreType.DMA((5,))]
         + [pltpu.SemaphoreType.DMA((GROUPS,))] * 2,
         compiler_params=pltpu.CompilerParams(
@@ -580,6 +570,7 @@
         cost_estimate=pl.CostEstimate(flops=60_000_000, bytes_accessed=1_200_000, transcendentals=0),
         name="cycle",
     )(right_side, phase)
+    return both[0], both[1]
 
 
 def solution(mesh):

time: 49.3 us -> 49.4 us (level)
  local copies, waits for them, and re-layouts: 1.49 us -> 0.95 us
  Pallas kernels: 47.1 us -> 47.6 us
    unnamed x2 -> x0, local copies, waits for them, and re-layouts: 1.49 us -> none
    squeeze x0 -> x1, local copies, waits for them, and re-layouts: none -> 0.95 us  [per_device(): return (both[0], both[1])]
    pallas_call x1, Pallas kernels: 47.1 us -> 47.6 us  [per_device(): pl.pallas_call(functools.partial(kernel, sizes), out_shape=pltpu.VMEM((2,...]
where the time goes in v5:
time: 49.4 us; the launch traced here: 49.2 us
  Pallas kernels  47.6 us (96%)
  local copies, waits for them, and re-layouts  0.95 us (2%)
  between operations  0.64 us (1%)
    pallas_call x1, Pallas kernels, per_device(): pl.pallas_call(functools.partial(kernel, sizes), out_shape=pltpu.VMEM((2,...  47.6 us

profile of v5, /device:TPU:1, one launch (start us, length us, event | category | flops | bytes accessed | tf_op | source)
XLA Modules:
  0.0 49.2 jit_solution(11996632602627139786)
XLA Ops:
  0.6 47.6 %cycle.1 = f32[2,12,12,512]{3,2,1,0:T(8,128)S(1)} custom-call(f32[12,12,512]{2,1,0:T(8,128)} %rhs.1, s32[12,12,512]{2,1,0:T(8,128)} %phase.1), custom_call_target="tpu_custom_call" | custom-call | flops 60000000 | bytes 1200000 | tf_op jit(solution)/shard_map/cycle/pallas_call | solution.py:554
  48.3 1.0 %slice_bitcast_fusion = (f32[12,12,512]{2,1,0:T(8,128)}, f32[12,12,512]{2,1,0:T(8,128)}) fusion(f32[2,12,12,512]{3,2,1,0:T(8,128)S(1)} %cycle.1), kind=kLoop, calls=%fused_computation | loop fusion | bytes 1179648 | tf_op jit(solution)/shard_map/squeeze | solution.py:573

commit v6 on v5

--- a/solution.py
+++ b/solution.py
@@ -197,26 +197,26 @@
     return guess * (2.0 - value * guess)
 
 
-def conduct(a, b, scale):
-    return scale * inverse_of(jnp.maximum(a + b, 0.5))
-
-
-def face_coefficients(rho, co, level, w, scale, unroll, tiles=None):
+def conduct(a, b):
+    return inverse_of(jnp.maximum(a + b, 0.25))
+
+
+def face_coefficients(rho, co, level, w, unroll, tiles=None):
     bx, by = co[:2]
     n, h = level["n"], level["h"]
     lo, hi, rows = h - w, h + n + w, n + 2 * w
     ts, ys, ends = slice(*(tiles or (0, level["t"]))), pl.ds(lo, rows), pl.ds(lo - 1, rows + 1)
 
     def body(i, c):
-        bx[i, ts, ys, :] = conduct(rho[i, ts, ys, :], rho[i + 1, ts, ys, :], scale)
-        by[i, ts, ends, :] = conduct(rho[i, ts, ends, :], rho[i, ts, pl.ds(lo, rows + 1), :], scale)
-        return c
-
-    bx[lo - 1, ts, ys, :] = conduct(rho[lo - 1, ts, ys, :], rho[lo, ts, ys, :], scale)
+        bx[i, ts, ys, :] = conduct(rho[i, ts, ys, :], rho[i + 1, ts, ys, :])
+        by[i, ts, ends, :] = conduct(rho[i, ts, ends, :], rho[i, ts, pl.ds(lo, rows + 1), :])
+        return c
+
+    bx[lo - 1, ts, ys, :] = conduct(rho[lo - 1, ts, ys, :], rho[lo, ts, ys, :])
     columns(lo, hi, unroll, body, 0)
 
 
-def other_coefficients(rho, co, level, w, scale, unroll):
+def other_coefficients(rho, co, level, w, unroll):
     bx, by, bzp, bzm, iv = co
     n, h = level["n"], level["h"]
     lo, hi, rows = h - w, h + n + w, n + 2 * w
@@ -224,7 +224,7 @@
 
     def body(i, c):
         here = rho[i, :, ys, :]
-        above = jnp.stack([conduct(a, b, scale) for a, b in zip(split(here), shifted(split(here), 1))])
+        above = jnp.stack([conduct(a, b) for a, b in zip(split(here), shifted(split(here), 1))])
         below = jnp.stack(shifted(split(above), -1))
         bzp[i, :, ys, :] = above
         bzm[i, :, ys, :] = below
@@ -235,9 +235,9 @@
     columns(lo, hi, unroll, body, 0)
 
 
-def coefficients(rho, co, level, w, scale, unroll):
-    face_coefficients(rho, co, level, w, scale, unroll)
-    other_coefficients(rho, co, level, w, scale, unroll)
+def coefficients(rho, co, level, w, unroll):
+    face_coefficients(rho, co, level, w, unroll)
+    other_coefficients(rho, co, level, w, unroll)
 
 
 def begin(r, iv, d, level, w, weight, unroll):
@@ -291,7 +291,7 @@
     sweep(v, co, level, w, unroll, finish)
 
 
-def restricted(fine, coarse, level_fine, level_coarse):
+def restricted(fine, coarse, level_fine, level_coarse, scale=0.125):
     h, n, hc = level_fine["h"], level_coarse["n"], level_coarse["h"]
 
     def body(i, c):
@@ -302,7 +302,7 @@
             both = fine[x, t, even, :] + fine[x, t, odd, :]
             both = both + (fine[x + 1, t, even, :] + fine[x + 1, t, odd, :])
             blocks.append(both)
-        coarse[hc + i, :, hc : hc + n, :] = jnp.stack(halved(blocks)) * 0.125
+        coarse[hc + i, :, hc : hc + n, :] = jnp.stack(halved(blocks)) * scale
         return c
 
     for i in range(n):
@@ -379,7 +379,7 @@
         density = []
         for t in range(4):
             part = slice(128 * t, 128 * t + 128)
-            density.append(jnp.where(kind[i, :, part] == 1, HEAVY, 1.0).astype(jnp.float32))
+            density.append(jnp.where(kind[i, :, part] == 1, 0.5 * HEAVY, 0.5).astype(jnp.float32))
             rho0[x, t, own, :] = density[t]
         zs_up[i, :12, :] = jnp.where(lane >= 64, r0[x, 3, own, :], pltpu.roll(density[3], 64, 1))
         zs_down[i, :12, :] = jnp.where(lane < 64, r0[x, 0, own, :], pltpu.roll(density[0], 64, 1))
@@ -426,16 +426,16 @@
     sender.exchange(fine_r, r0, l0, 4, CORNERS, cut=True)
     sender.exchange(fine_r, r0, l0, 4, FACES, (4, 5))
 
-    restricted(rho0, rho1, l0, l1)
-    restricted(rho1, rho2, l1, l2)
+    restricted(rho0, rho1, l0, l1, 0.5)
+    restricted(rho1, rho2, l1, l2, 0.5)
     density1 = sender.exchange(sender.group(), rho1, l1, 7, diamond(6, 7, 2), zeros=zeros)
     density2 = sender.exchange(sender.group(), rho2, l2, 8, line_y2, zeros=zeros)
 
     fine_rho.wait_recv()
-    face_coefficients(rho0, co0, l0, 4, 2.0, 2, (0, 4))
+    face_coefficients(rho0, co0, l0, 4, 4, (0, 4))
     fine_rho4.wait_recv()
-    face_coefficients(rho0, co0, l0, 4, 2.0, 5, (4, 5))
-    other_coefficients(rho0, co0, l0, 4, 2.0, 2)
+    face_coefficients(rho0, co0, l0, 4, 5, (4, 5))
+    other_coefficients(rho0, co0, l0, 4, 4)
     fine_r.wait_recv()
     fine_r.wait_send()
     begin(r0, co0[4], d01, l0, 4, first, 4)
@@ -455,7 +455,7 @@
     density2x = sender.exchange(sender.group(), rho2, l2, 8, line_x2, whole_y=True, zeros=zeros)
     density1.wait_recv()
     density1.wait_send()
-    coefficients(rho1, co1, l1, 6, 0.5, 2)
+    coefficients(rho1, co1, l1, 6, 3)
     back0 = sender.exchange(sender.group(), up0, l0, 4, AROUND)
     second.wait_recv()
     second.wait_send()
@@ -475,7 +475,7 @@
     density2x.wait_recv()
     density2.wait_send()
     density2x.wait_send()
-    coefficients(rho2, co2, l2, 7, 0.125, 2)
+    coefficients(rho2, co2, l2, 7, 4)
     back1 = sender.exchange(sender.group(), up1, l1, 6, AROUND)
     sender.exchange(back1, x1, l1, 3, AROUND, zeros=zeros)
     third.wait_recv()

time: 49.4 us -> 48.3 us (0.978)
  Pallas kernels: 47.6 us -> 46.6 us
    pallas_call x1, Pallas kernels: 47.6 us -> 46.6 us  [per_device(): pl.pallas_call(functools.partial(kernel, sizes), out_shape=pltpu.VMEM((2,...]
where the time goes in v6:
time: 48.3 us; the launch traced here: 48.1 us
  Pallas kernels  46.6 us (96%)
  local copies, waits for them, and re-layouts  0.95 us (2%)
  between operations  0.64 us (1%)
    pallas_call x1, Pallas kernels, per_device(): pl.pallas_call(functools.partial(kernel, sizes), out_shape=pltpu.VMEM((2,...  46.6 us

profile of v6, /device:TPU:1, one launch (start us, length us, event | category | flops | bytes accessed | tf_op | source)
XLA Modules:
  0.0 48.1 jit_solution(10636990300362615106)
XLA Ops:
  0.6 46.6 %cycle.1 = f32[2,12,12,512]{3,2,1,0:T(8,128)S(1)} custom-call(f32[12,12,512]{2,1,0:T(8,128)} %rhs.1, s32[12,12,512]{2,1,0:T(8,128)} %phase.1), custom_call_target="tpu_custom_call" | custom-call | flops 60000000 | bytes 1200000 | tf_op jit(solution)/shard_map/cycle/pallas_call | solution.py:554
  47.2 1.0 %slice_bitcast_fusion = (f32[12,12,512]{2,1,0:T(8,128)}, f32[12,12,512]{2,1,0:T(8,128)}) fusion(f32[2,12,12,512]{3,2,1,0:T(8,128)S(1)} %cycle.1), kind=kLoop, calls=%fused_computation | loop fusion | bytes 1179648 | tf_op jit(solution)/shard_map/squeeze | solution.py:573
